TPU v7x, 32 devices: a whole 2x2x4 slice. The times are simulated.
32 devices in a mesh: blk: 2 (over y), dp: 16 (over z, x, core).
Axes of the slice: x: 2, y: 2, z: 4, core: 2. Of those that a mesh axis runs over, the one named last changes fastest.
Arguments:
- inputs: bfloat16 [64, 512, 768], P('dp', 'blk'), may hold values from -6 to 6
- cotangent: bfloat16 [64, 512, 768], P('dp', 'blk'), may hold values from -6 to 6
- flags: int32 [64, 2048], P('dp', 'blk'), may hold values 0 or 1
- gain_one: float32 [768], replicated, may hold values from 0.25 to 1.75
- shift_one: float32 [768], replicated, may hold values from -1.5 to 1.5
- query_weight: bfloat16 [768, 768], replicated, may hold values from -0.21875 to 0.21875
- query_bias: float32 [768], replicated, may hold values from -1.5 to 1.5
- key_weight: bfloat16 [768, 768], replicated, may hold values from -0.21875 to 0.21875
- value_weight: bfloat16 [768, 768], replicated, may hold values from -0.21875 to 0.21875
- value_bias: float32 [768], replicated, may hold values from -1.5 to 1.5
- proj_weight: bfloat16 [768, 768], replicated, may hold values from -0.875 to 0.875
- proj_bias: float32 [768], replicated, may hold values from -1.5 to 1.5
- gain_two: float32 [768], replicated, may hold values from 0.25 to 1.75
- shift_two: float32 [768], replicated, may hold values from -1.5 to 1.5
- inner_weight: bfloat16 [768, 3072], replicated, may hold values from -0.21875 to 0.21875
- inner_bias: float32 [3072], replicated, may hold values from -1.5 to 1.5
- outer_weight: bfloat16 [3072, 768], replicated, may hold values from -0.109375 to 0.109375
- outer_bias: float32 [768], replicated, may hold values from -1.5 to 1.5
Outputs:
- output: bfloat16 [64, 512, 768], P('dp', 'blk')
- input_grad: bfloat16 [64, 512, 768], P('dp', 'blk')
- gain_one_grad: float32 [768], replicated
- shift_one_grad: float32 [768], replicated
- query_weight_grad: float32 [768, 768], replicated
- query_bias_grad: float32 [768], replicated
- key_weight_grad: float32 [768, 768], replicated
- value_weight_grad: float32 [768, 768], replicated
- value_bias_grad: float32 [768], replicated
- proj_weight_grad: float32 [768, 768], replicated
- proj_bias_grad: float32 [768], replicated
- gain_two_grad: float32 [768], replicated
- shift_two_grad: float32 [768], replicated
- inner_weight_grad: float32 [768, 3072], replicated
- inner_bias_grad: float32 [3072], replicated
- outer_weight_grad: float32 [3072, 768], replicated
- outer_bias_grad: float32 [768], replicated
All inputs are finite; a program needn't handle non-finite values. No bound on the sum of `flags` on one device may be relied on, other than what follows from the above.
Results may differ from a plain program's by a relative error of at most 0.014.
Values may be sent and summed in bfloat16 or wider, within the bound.
No kernel may reach another device: no remote copies, remote signals or barrier semaphores. Data moves between devices by JAX's collectives and lax.ppermute only.
A program may use at most 256 MiB of HBM per device.

v0:
```python
import jax
import jax.numpy as jnp
from jax import lax
from jax.sharding import PartitionSpec as P

HEADS = 12
MICRO = 2


EPS = 1e-05


def shortened(shard):
    return jax.tree.map(lambda a: a.astype(jnp.bfloat16) if a.dtype == jnp.float32 else a, shard)


def normalize(values):
    center = values - jnp.mean(values, axis=-1, keepdims=True)
    scale = lax.rsqrt(jnp.mean(center * center, axis=-1, keepdims=True) + EPS)
    return (center * scale, scale)


def norm_back(grad, unit, scale, gain):
    scaled = grad * gain
    return scale * (
        scaled
        - jnp.mean(scaled, axis=-1, keepdims=True)
        - unit * jnp.mean(scaled * unit, axis=-1, keepdims=True)
    )


def matmul(left, right):
    return jnp.einsum("rnd,de->rne", left, right, preferred_element_type=jnp.float32)


def back_mul(left, right):
    return jnp.einsum("rne,de->rnd", left, right, preferred_element_type=jnp.float32)


def outer_sum(left, right):
    return jnp.einsum("rnd,rne->de", left, right, preferred_element_type=jnp.float32)


def column_sum(grad):
    return jnp.sum(grad.astype(jnp.float32), axis=(0, 1))


def gelu_slope(values):
    return (
        0.5 * (1.0 + lax.erf(values * 0.7071067811865476))
        + values * jnp.exp(-0.5 * values * values) * 0.3989422804014327
    )


def layer_pass(inputs, grad_low, params):
    (
        gain_one,
        shift_one,
        query_weight,
        query_bias,
        key_weight,
        value_weight,
        value_bias,
        proj_weight,
        proj_bias,
        gain_two,
        shift_two,
        inner_weight,
        inner_bias,
        outer_weight,
        outer_bias,
    ) = params
    batch, local, width = inputs.shape
    head_size = width // HEADS
    factor = head_size ** (-0.5)
    hidden = inputs.astype(jnp.float32)
    unit_one, scale_one = normalize(hidden)
    first = (unit_one * gain_one + shift_one).astype(jnp.bfloat16)
    query = (matmul(first, query_weight) + query_bias).astype(jnp.bfloat16)
    key = matmul(first, key_weight).astype(jnp.bfloat16)
    value = (matmul(first, value_weight) + value_bias).astype(jnp.bfloat16)
    keys_row, values_row = (
        lax.all_gather(key, "blk", axis=1, tiled=True),
        lax.all_gather(value, "blk", axis=1, tiled=True),
    )
    length = keys_row.shape[1]
    query_heads = query.reshape(batch, local, HEADS, head_size)
    key_heads = keys_row.reshape(batch, length, HEADS, head_size)
    value_heads = values_row.reshape(batch, length, HEADS, head_size)
    scores = (
        jnp.einsum("rqhc,rkhc->rhqk", query_heads, key_heads, preferred_element_type=jnp.float32)
        * factor
    )
    weights = jnp.exp(scores - jnp.max(scores, axis=-1, keepdims=True))
    probs = weights / jnp.sum(weights, axis=-1, keepdims=True)
    probs_low = probs.astype(jnp.bfloat16)
    mixed = jnp.einsum(
        "rhqk,rkhc->rqhc", probs_low, value_heads, preferred_element_type=jnp.float32
    )
    mixed = mixed.reshape(batch, local, width).astype(jnp.bfloat16)
    resid = hidden + (matmul(mixed, proj_weight) + proj_bias)
    unit_two, scale_two = normalize(resid)
    second = (unit_two * gain_two + shift_two).astype(jnp.bfloat16)
    inner = matmul(second, inner_weight) + inner_bias
    act = jax.nn.gelu(inner, approximate=False).astype(jnp.bfloat16)
    output = (resid + matmul(act, outer_weight) + outer_bias).astype(jnp.bfloat16)
    grad_out = grad_low.astype(jnp.float32)
    outer_weight_grad = outer_sum(act, grad_low)
    outer_bias_grad = column_sum(grad_out)
    grad_inner = (back_mul(grad_low, outer_weight) * gelu_slope(inner)).astype(jnp.bfloat16)
    inner_weight_grad = outer_sum(second, grad_inner)
    inner_bias_grad = column_sum(grad_inner)
    grad_second = back_mul(grad_inner, inner_weight)
    gain_two_grad = jnp.sum(grad_second * unit_two, axis=(0, 1))
    shift_two_grad = jnp.sum(grad_second, axis=(0, 1))
    grad_resid = grad_out + norm_back(grad_second, unit_two, scale_two, gain_two)
    grad_branch = grad_resid.astype(jnp.bfloat16)
    proj_weight_grad = outer_sum(mixed, grad_branch)
    proj_bias_grad = column_sum(grad_branch)
    grad_mixed = (
        back_mul(grad_branch, proj_weight)
        .astype(jnp.bfloat16)
        .reshape(batch, local, HEADS, head_size)
    )
    grad_probs = jnp.einsum(
        "rqhc,rkhc->rhqk", grad_mixed, value_heads, preferred_element_type=jnp.float32
    )
    value_terms = jnp.einsum(
        "rhqk,rqhc->rkhc", probs_low, grad_mixed, preferred_element_type=jnp.float32
    )
    value_terms = value_terms.reshape(batch, length, width)
    grad_scores = (
        probs * (grad_probs - jnp.sum(probs * grad_probs, axis=-1, keepdims=True))
    ).astype(jnp.bfloat16)
    grad_query = (
        jnp.einsum("rhqk,rkhc->rqhc", grad_scores, key_heads, preferred_element_type=jnp.float32)
        * factor
    )
    grad_query = grad_query.reshape(batch, local, width).astype(jnp.bfloat16)
    key_terms = (
        jnp.einsum("rhqk,rqhc->rkhc", grad_scores, query_heads, preferred_element_type=jnp.float32)
        * factor
    )
    key_terms = key_terms.reshape(batch, length, width)
    grad_key, grad_value = (
        lax.psum_scatter(
            key_terms.astype(jnp.bfloat16), "blk", scatter_dimension=1, tiled=True
        ).astype(jnp.float32),
        lax.psum_scatter(
            value_terms.astype(jnp.bfloat16), "blk", scatter_dimension=1, tiled=True
        ).astype(jnp.float32),
    )
    grad_key = grad_key.astype(jnp.bfloat16)
    grad_value = grad_value.astype(jnp.bfloat16)
    query_weight_grad = outer_sum(first, grad_query)
    query_bias_grad = column_sum(grad_query)
    key_weight_grad = outer_sum(first, grad_key)
    value_weight_grad = outer_sum(first, grad_value)
    value_bias_grad = column_sum(grad_value)
    grad_first = (
        back_mul(grad_query, query_weight)
        + back_mul(grad_key, key_weight)
        + back_mul(grad_value, value_weight)
    )
    gain_one_grad = jnp.sum(grad_first * unit_one, axis=(0, 1))
    shift_one_grad = jnp.sum(grad_first, axis=(0, 1))
    input_grad = (grad_resid + norm_back(grad_first, unit_one, scale_one, gain_one)).astype(
        jnp.bfloat16
    )
    matrices = (
        query_weight_grad,
        key_weight_grad,
        value_weight_grad,
        proj_weight_grad,
        inner_weight_grad,
        outer_weight_grad,
    )
    vectors = (
        gain_one_grad,
        shift_one_grad,
        query_bias_grad,
        value_bias_grad,
        proj_bias_grad,
        gain_two_grad,
        shift_two_grad,
        outer_bias_grad,
        inner_bias_grad,
    )
    return (output, input_grad, matrices, vectors)


def reduce_terms(terms):
    return lax.psum_scatter(terms, ("blk", "dp"), scatter_dimension=0, tiled=True)


def gather_terms(shares):
    return jax.tree.map(
        lambda part, own: part.astype(own.dtype),
        lax.all_gather(shortened(shares), ("blk", "dp"), axis=0, tiled=True),
        shares,
    )


def on_device(
    inputs,
    cotangent,
    flags,
    gain_one,
    shift_one,
    query_weight,
    query_bias,
    key_weight,
    value_weight,
    value_bias,
    proj_weight,
    proj_bias,
    gain_two,
    shift_two,
    inner_weight,
    inner_bias,
    outer_weight,
    outer_bias,
):
    params = (
        gain_one,
        shift_one,
        query_weight,
        query_bias,
        key_weight,
        value_weight,
        value_bias,
        proj_weight,
        proj_bias,
        gain_two,
        shift_two,
        inner_weight,
        inner_bias,
        outer_weight,
        outer_bias,
    )
    batch, local, width = inputs.shape
    masked = jnp.max(flags.reshape(batch, local, -1), axis=-1).astype(jnp.float32)
    masked_grad = (cotangent.astype(jnp.float32) * masked[:, :, None]).astype(jnp.bfloat16)
    share = batch // MICRO
    outputs = []
    input_grads = []
    totals = None
    for number in range(MICRO):
        lower = number * share
        upper = lower + share
        part_in = inputs[lower:upper]
        part_grad = masked_grad[lower:upper]
        output, input_grad, matrices, vectors = layer_pass(part_in, part_grad, params)
        terms = tuple((matrix.reshape(-1) for matrix in matrices)) + (jnp.concatenate(vectors),)
        totals = terms if totals is None else jax.tree.map(jnp.add, totals, terms)
        outputs.append(output)
        input_grads.append(input_grad)
    whole = gather_terms(reduce_terms(totals))
    query_weight_grad = whole[0].reshape(query_weight.shape)
    key_weight_grad = whole[1].reshape(key_weight.shape)
    value_weight_grad = whole[2].reshape(value_weight.shape)
    proj_weight_grad = whole[3].reshape(proj_weight.shape)
    inner_weight_grad = whole[4].reshape(inner_weight.shape)
    outer_weight_grad = whole[5].reshape(outer_weight.shape)
    packed = whole[6]
    gain_one_grad = packed[0:width]
    shift_one_grad = packed[width : 2 * width]
    query_bias_grad = packed[2 * width : 3 * width]
    value_bias_grad = packed[3 * width : 4 * width]
    proj_bias_grad = packed[4 * width : 5 * width]
    gain_two_grad = packed[5 * width : 6 * width]
    shift_two_grad = packed[6 * width : 7 * width]
    outer_bias_grad = packed[7 * width : 8 * width]
    inner_bias_grad = packed[8 * width :]
    return (
        jnp.concatenate(outputs, axis=0),
        jnp.concatenate(input_grads, axis=0),
        gain_one_grad,
        shift_one_grad,
        query_weight_grad,
        query_bias_grad,
        key_weight_grad,
        value_weight_grad,
        value_bias_grad,
        proj_weight_grad,
        proj_bias_grad,
        gain_two_grad,
        shift_two_grad,
        inner_weight_grad,
        inner_bias_grad,
        outer_weight_grad,
        outer_bias_grad,
    )


def solution(mesh):
    in_specs = (
        P("dp", "blk", None),
        P("dp", "blk", None),
        P("dp", "blk"),
        P(),
        P(),
        P(),
        P(),
        P(),
        P(),
        P(),
        P(),
        P(),
        P(),
        P(),
        P(),
        P(),
        P(),
        P(),
    )
    out_specs = (
        P("dp", "blk", None),
        P("dp", "blk", None),
        P(),
        P(),
        P(),
        P(),
        P(),
        P(),
        P(),
        P(),
        P(),
        P(),
        P(),
        P(),
        P(),
        P(),
        P(),
    )
    return jax.shard_map(
        on_device, mesh=mesh, in_specs=in_specs, out_specs=out_specs, check_vma=False
    )
```

profile of v0, /device:TPU:0, one launch (start us, length us, event | category | flops | bytes accessed | tf_op | source)
XLA Modules:
  0.0 1237.6 jit_solution(5932244027408122941)
XLA Ops:
  13.6 3.1 convolution_convert_fusion.3
  28.1 2.9 multiply_convert_fusion.4
  30.9 10.8 all-gather.17.cloned.1.call-done
  41.7 2.9 copy.105
  44.6 10.7 fusion.164
  55.3 15.8 %all-gather.15.cloned.1.call-done = bf16[2,512,768]{2,1,0:T(8,128)(2,1)} async-done(((bf16[2,256,768]{2,1,0:T(8,128)(2,1)}), bf16[2,512,768]{2,1,0:T(8,128)(2,1)}) %all-gather.15.cloned.1.call-update) | async-done | bytes 1572880 | tf_op jit(solution)/shard_map/all_gather | solution.py:84
  73.7 6.5 fusion.110
  83.0 17.4 %all-gather.13.cloned.1.call-done = bf16[2,512,768]{2,1,0:T(8,128)(2,1)} async-done(((bf16[2,256,768]{2,1,0:T(8,128)(2,1)}), bf16[2,512,768]{2,1,0:T(8,128)(2,1)}) %all-gather.13.cloned.1.call-update) | async-done | bytes 1572880 | tf_op jit(solution)/shard_map/all_gather | solution.py:83
  104.8 10.3 fusion.165
  115.1 14.6 %all-gather.11.cloned.1.call-done = bf16[2,512,768]{2,1,0:T(8,128)(2,1)} async-done(((bf16[2,256,768]{2,1,0:T(8,128)(2,1)}), bf16[2,512,768]{2,1,0:T(8,128)(2,1)}) %all-gather.11.cloned.1.call-update) | async-done | bytes 1572880 | tf_op jit(solution)/shard_map/all_gather | solution.py:84
  132.3 6.9 fusion.107
  142.2 4.7 fusion.51
  146.9 15.6 %fusion.101 = (u8[256,3072]{1,0:T(8,128)(4,1)}, u8[256,3072]{1,0:T(8,128)(4,1)}, u8[256,3072]{1,0:T(8,128)(4,1)}, u8[256,3072]{1,0:T(8,128)(4,1)}, f32[2,256,3072]{2,1,0:T(8,128)}) fusion(f32[3072]{0:T(1024)S(1)} %copy-done.63, f32[2,256,3072]{2,1,0:T(8,128)S(1)} %fusion.51, bf16[768,3072]{1,0:T(8,128)(2,1)} %param.32, ...), kind=kOutput, calls=%fused_computation.177 | convolution fusion | flops 2458779648 | bytes 22042624 | tf_op jit(solution)/shard_map/rnd,de->rne/dot_general | solution.py:33
  162.6 7.0 convert_reduce_fusion
  169.5 6.2 fusion.47
  175.7 6.9 convert_reduce_fusion.1
  182.6 4.0 multiply_reduce_fusion.5
  186.7 3.1 convert_reduce_fusion.4
  194.9 11.2 multiply_reduce_fusion
  208.2 6.1 multiply_convert_fusion
  214.3 3.0 multiply_convert_fusion.2
  220.3 3.4 convolution_convert_fusion.1
  226.1 11.3 multiply_reduce_fusion.1
  239.5 6.0 multiply_convert_fusion.1
  245.5 2.9 multiply_convert_fusion.3
  252.5 6.7 fusion.78
  259.2 2.6 copy.114
  261.9 6.8 fusion.75
  269.1 6.9 convert_reduce_fusion.11
  276.0 2.7 copy.110
  278.6 3.8 fusion.152
  287.1 2.7 convert_reduce_fusion.8
  289.8 2.9 fusion.140
  292.8 5.7 fusion.4
  298.8 32.8 %fusion.11 = (bf16[2,256,3072]{2,1,0:T(8,128)(2,1)}, bf16[2,256,3072]{2,1,0:T(8,128)(2,1)}) fusion(f32[2,256,3072]{2,1,0:T(8,128)} %get-tuple-element.88, f32[3072]{0:T(1024)} %param.33, u8[256,3072]{1,0:T(8,128)(4,1)} %get-tuple-element.18, u8[256,3072]{1,0:T(8,128)(4,1)} %get-tuple-element.17, u8[256,3072]{1,0:T(8,128)(4,1)} %get-tuple-element.45, ...), kind=kLoop, calls=%fused_computation.21 | loop fusion | flops 221773824 | bytes 22032384 | tf_op jit(solution)/shard_map/convert_element_type | solution.py:105
  336.9 3.2 add.282
  340.1 3.2 add.288
  343.3 9.8 copy.143
  353.1 2.7 fusion.138
  355.8 5.4 bitcast_add_fusion
  361.2 11.0 add.292
  372.2 3.4 fusion.127
  377.5 3.5 fusion.121
  381.0 3.5 fusion.123
  384.5 4.1 add_add_fusion
  388.6 5.9 fusion.97
  399.6 3.2 add.284
  407.4 3.2 add.286
  410.6 456.4 %all-reduce.10 = (bf16[9216]{0:T(1024)(128)(2,1)S(1)}, bf16[589824]{0:T(1024)(128)(2,1)}, bf16[589824]{0:T(1024)(128)(2,1)}, bf16[589824]{0:T(1024)(128)(2,1)}, ...) all-reduce(f32[9216]{0:T(1024)S(1)} %copy-done.33, ...), channel_id=6, replica_groups=mesh['blk'=2,'dp'=16] {'blk','dp'}, use_global_device_ids=true, to_apply=%region_45.0.clone | all-reduce | flops 7087104 | bytes 42522624
  876.2 6.5 add_convert_fusion
  882.7 5.0 add_convert_fusion.4
  889.3 38.8 %all-reduce = bf16[9216]{0:T(1024)(128)(2,1)S(1)} all-reduce(bf16[9216]{0:T(1024)(128)(2,1)S(1)} %dynamic-update-slice), channel_id=1, replica_groups=mesh['blk'=2,'dp'=16] {'blk','dp'}, use_global_device_ids=true, to_apply=%add | all-reduce | flops 9216 | bytes 36864
  928.8 3.5 fusion.96
  934.2 3.3 reshape.253
  937.5 39.5 %all-gather.21.cloned.1.call-done = bf16[589824]{0:T(1024)(128)(2,1)} async-done(((bf16[18432]{0:T(1024)(128)(2,1)}), bf16[589824]{0:T(1024)(128)(2,1)}) %all-gather.21.cloned.1.call-update) | async-done | bytes 1179664 | tf_op jit(solution)/shard_map/all_gather | solution.py:199
  977.0 3.3 reshape.255
  980.4 53.1 %all-gather.23.cloned.1.call-done = bf16[589824]{0:T(1024)(128)(2,1)} async-done(((bf16[18432]{0:T(1024)(128)(2,1)}), bf16[589824]{0:T(1024)(128)(2,1)}) %all-gather.23.cloned.1.call-update) | async-done | bytes 1179664 | tf_op jit(solution)/shard_map/all_gather | solution.py:199
  1033.4 3.3 reshape.257
  1036.8 52.3 %all-gather.25.cloned.1.call-done = bf16[589824]{0:T(1024)(128)(2,1)} async-done(((bf16[18432]{0:T(1024)(128)(2,1)}), bf16[589824]{0:T(1024)(128)(2,1)}) %all-gather.25.cloned.1.call-update) | async-done | bytes 1179664 | tf_op jit(solution)/shard_map/all_gather | solution.py:199
  1089.1 3.3 reshape.259
  1092.5 62.7 %all-gather.27.cloned.1.call-done = bf16[2359296]{0:T(1024)(128)(2,1)} async-done(((bf16[73728]{0:T(1024)(128)(2,1)}), bf16[2359296]{0:T(1024)(128)(2,1)}) %all-gather.27.cloned.1.call-update) | async-done | bytes 4718608 | tf_op jit(solution)/shard_map/all_gather | solution.py:199
  1155.1 8.7 reshape.261
  1163.9 57.0 %all-gather.29.cloned.1.call-done = bf16[2359296]{0:T(1024)(128)(2,1)} async-done(((bf16[73728]{0:T(1024)(128)(2,1)}), bf16[2359296]{0:T(1024)(128)(2,1)}) %all-gather.29.cloned.1.call-update) | async-done | bytes 4718608 | tf_op jit(solution)/shard_map/all_gather | solution.py:199
  1220.9 10.0 reshape.263
  (328 shorter events, 86.6 us)
Async XLA Ops:
  7.2 34.5 %all-gather.17.cloned.1.call-start = ((), (), s32[]{:S(2)}) async-start(), calls=%async_computation.7 | async-start | bytes 2359296 | tf_op jit(solution)/shard_map/all_gather | solution.py:83
  9.1 7.7 copy-start.52
  9.1 9.6 copy-start.35
  9.8 8.9 copy-start.40
  11.7 59.4 %all-gather.15.cloned.1.call-start = ((), (), s32[]{:S(2)}) async-start(), calls=%async_computation.6 | async-start | bytes 2359296 | tf_op jit(solution)/shard_map/all_gather | solution.py:84
  13.6 86.9 %all-gather.13.cloned.1.call-start = ((), (), s32[]{:S(2)}) async-start(), calls=%async_computation.5 | async-start | bytes 2359296 | tf_op jit(solution)/shard_map/all_gather | solution.py:83
  16.7 112.9 %all-gather.11.cloned.1.call-start = ((), (), s32[]{:S(2)}) async-start(), calls=%async_computation.4 | async-start | bytes 2359296 | tf_op jit(solution)/shard_map/all_gather | solution.py:84
  18.6 358.9 %reduce-scatter.9.cloned.1.call-start = ((), (), s32[]{:S(2)}) async-start(), calls=%async_computation.10 | async-start | bytes 2359296 | tf_op jit(solution)/shard_map/reduce_scatter | solution.py:146
  73.7 7.4 copy-start.80
  73.7 7.4 copy-start.89
  104.8 81.8 %copy-start.46 = (f32[2,256]{1,0:T(2,128)}, f32[2,256]{1,0:T(2,128)S(1)}, u32[]{:S(2)}) copy-start(f32[2,256]{1,0:T(2,128)S(1)} %add_rsqrt_fusion) | copy-start | bytes 6148
  132.3 6.9 copy-start.81
  140.1 46.5 %copy-start.12 = (f32[2,256,768]{2,1,0:T(8,128)}, f32[2,256,768]{2,1,0:T(8,128)S(1)}, u32[]{:S(2)}) copy-start(f32[2,256,768]{2,1,0:T(8,128)S(1)} %get-tuple-element.85) | copy-start | bytes 4718596
  140.2 46.4 %copy-start.50 = (f32[2,256]{1,0:T(2,128)}, f32[2,256]{1,0:T(2,128)S(1)}, u32[]{:S(2)}) copy-start(f32[2,256]{1,0:T(2,128)S(1)} %broadcast_multiply_fusion.10) | copy-start | bytes 6148
  142.1 44.5 %copy-start.70 = (f32[2,256]{1,0:T(2,128)}, f32[2,256]{1,0:T(2,128)S(1)}, u32[]{:S(2)}) copy-start(f32[2,256]{1,0:T(2,128)S(1)} %add_rsqrt_fusion.2) | copy-start | bytes 6148
  146.9 15.6 %copy-start.16 = (f32[2,256,3072]{2,1,0:T(8,128)}, f32[2,256,3072]{2,1,0:T(8,128)S(1)}, u32[]{:S(2)}) copy-start(f32[2,256,3072]{2,1,0:T(8,128)S(1)} %fusion.51) | copy-start | bytes 18874372
  146.9 15.6 %copy-start.9 = (bf16[4,256,768]{2,1,0:T(8,128)(2,1)S(1)}, bf16[4,256,768]{2,1,0:T(8,128)(2,1)}, u32[]{:S(2)}) copy-start(bf16[4,256,768]{2,1,0:T(8,128)(2,1)} %multiply_convert_fusion.4) | copy-start | bytes 4718596
  169.5 6.2 copy-start.18
  169.5 6.2 copy-start.17
  169.5 13.1 %slice-start.8 = ((s8[4718592]{0:T(1024)(128)(4,1)}), s8[4194304]{0:T(1024)(128)(4,1)S(1)}, s32[]{:S(2)}) async-start(s8[4718592]{0:T(1024)(128)(4,1)} %bitcast.218), calls=%async_computation.26 | async-start | bytes 8388608
  175.7 6.9 slice-start.9
  194.9 11.3 slice-start.2
  194.9 11.8 slice-start.3
  194.9 13.3 %slice-start.4 = ((s8[12582912]{0:T(1024)(128)(4,1)}), s8[4194304]{0:T(1024)(128)(4,1)S(1)}, s32[]{:S(2)}) async-start(s8[12582912]{0:T(1024)(128)(4,1)} %bitcast.186), calls=%async_computation.22 | async-start | bytes 8388608
  194.9 13.3 %copy-start.48 = (f32[2,12,256]{2,1,0:T(8,128)S(1)}, f32[2,12,256]{2,1,0:T(8,128)}, u32[]{:S(2)}) copy-start(f32[2,12,256]{2,1,0:T(8,128)} %get-tuple-element.80) | copy-start | bytes 73732
  220.0 161.0 %reduce-scatter.5.cloned.1.call-start = ((), (), s32[]{:S(2)}) async-start(), calls=%async_computation.8 | async-start | bytes 2359296 | tf_op jit(solution)/shard_map/reduce_scatter | solution.py:146
  226.0 11.3 slice-start.5
  226.0 12.0 slice-start.6
  226.0 13.5 %slice-start.7 = ((s8[12582912]{0:T(1024)(128)(4,1)}), s8[4194304]{0:T(1024)(128)(4,1)S(1)}, s32[]{:S(2)}) async-start(s8[12582912]{0:T(1024)(128)(4,1)} %bitcast.188), calls=%async_computation.25 | async-start | bytes 8388608
  226.0 13.5 %copy-start.49 = (f32[2,12,256]{2,1,0:T(8,128)S(1)}, f32[2,12,256]{2,1,0:T(8,128)}, u32[]{:S(2)}) copy-start(f32[2,12,256]{2,1,0:T(8,128)} %get-tuple-element.82) | copy-start | bytes 73732
  251.4 133.1 %reduce-scatter.11.cloned.1.call-start = ((), (), s32[]{:S(2)}) async-start(), calls=%async_computation.11 | async-start | bytes 2359296 | tf_op jit(solution)/shard_map/reduce_scatter | solution.py:149
  268.7 119.9 %reduce-scatter.7.cloned.1.call-start = ((), (), s32[]{:S(2)}) async-start(), calls=%async_computation.9 | async-start | bytes 2359296 | tf_op jit(solution)/shard_map/reduce_scatter | solution.py:149
  276.0 6.5 copy-start.27
  278.6 8.4 slice-start
  298.5 635.6 %all-gather.19.cloned.1.call-start = ((), (), s32[]{:S(2)}) async-start(), calls=%async_computation.12 | async-start | bytes 1216512 | tf_op jit(solution)/shard_map/all_gather | solution.py:199
  298.8 32.9 %copy-start.23 = (f32[768,768,1]{1,0,2:T(8,128)S(1)}, f32[768,768,1]{1,0,2:T(8,128)}, u32[]{:S(2)}) copy-start(f32[768,768,1]{1,0,2:T(8,128)} %fusion.152) | copy-start | bytes 7077892
  298.8 32.9 %copy-start.36 = (f32[2,256]{1,0:T(2,128)S(1)}, f32[2,256]{1,0:T(2,128)}, u32[]{:S(2)}) copy-start(f32[2,256]{1,0:T(2,128)} %copy-done.35) | copy-start | bytes 6148
  298.8 32.9 %copy-start.41 = (f32[2,256]{1,0:T(2,128)S(1)}, f32[2,256]{1,0:T(2,128)}, u32[]{:S(2)}) copy-start(f32[2,256]{1,0:T(2,128)} %copy-done.40) | copy-start | bytes 6148
  298.8 32.9 %copy-start.45 = (f32[768]{0:T(1024)S(1)}, f32[768]{0:T(1024)}, u32[]{:S(2)}) copy-start(f32[768]{0:T(1024)} %param.22) | copy-start | bytes 9220
  343.3 9.8 copy-start.10
  343.3 9.8 copy-start.21
  388.5 6.5 copy-start.11
  388.5 6.1 copy-start.29
  388.6 6.3 copy-start.59
  388.6 6.3 copy-start.75
  388.6 6.3 copy-start.74
  388.6 6.3 copy-start.58
  388.6 6.3 copy-start.65
  388.6 6.3 copy-start.42
  388.6 6.4 copy-start.61
  410.6 465.6 %copy-start.90 = (f32[768]{0:T(1024)S(1)}, f32[768]{0:T(1024)}, u32[]{:S(2)}) copy-start(f32[768]{0:T(1024)} %param.35) | copy-start | bytes 9220
  868.4 108.6 %all-gather.21.cloned.1.call-start = ((), (), s32[]{:S(2)}) async-start(), calls=%async_computation.13 | async-start | bytes 1216512 | tf_op jit(solution)/shard_map/all_gather | solution.py:199
  869.9 163.5 %all-gather.23.cloned.1.call-start = ((), (), s32[]{:S(2)}) async-start(), calls=%async_computation.14 | async-start | bytes 1216512 | tf_op jit(solution)/shard_map/all_gather | solution.py:199
  871.4 217.8 %all-gather.25.cloned.1.call-start = ((), (), s32[]{:S(2)}) async-start(), calls=%async_computation.15 | async-start | bytes 1216512 | tf_op jit(solution)/shard_map/all_gather | solution.py:199
  872.8 282.3 %all-gather.27.cloned.1.call-start = ((), (), s32[]{:S(2)}) async-start(), calls=%async_computation.16 | async-start | bytes 4866048 | tf_op jit(solution)/shard_map/all_gather | solution.py:199
  874.5 346.4 %all-gather.29.cloned.1.call-start = ((), (), s32[]{:S(2)}) async-start(), calls=%async_computation.17 | async-start | bytes 4866048 | tf_op jit(solution)/shard_map/all_gather | solution.py:199
  876.2 6.5 copy-start.14
  876.2 6.5 copy-start.22
  887.7 41.0 %copy-start.79 = (f32[2,256]{1,0:T(2,128)S(1)}, f32[2,256]{1,0:T(2,128)}, u32[]{:S(2)}) copy-start(f32[2,256]{1,0:T(2,128)} %get-tuple-element.28) | copy-start | bytes 6148
  887.7 41.0 %copy-start.78 = (f32[2,256]{1,0:T(2,128)S(1)}, f32[2,256]{1,0:T(2,128)}, u32[]{:S(2)}) copy-start(f32[2,256]{1,0:T(2,128)} %get-tuple-element.32) | copy-start | bytes 6148
  887.7 41.0 %copy-start.77 = (f32[2,256]{1,0:T(2,128)S(1)}, f32[2,256]{1,0:T(2,128)}, u32[]{:S(2)}) copy-start(f32[2,256]{1,0:T(2,128)} %get-tuple-element.29) | copy-start | bytes 6148
  887.7 41.1 %copy-start.76 = (f32[2,256]{1,0:T(2,128)S(1)}, f32[2,256]{1,0:T(2,128)}, u32[]{:S(2)}) copy-start(f32[2,256]{1,0:T(2,128)} %get-tuple-element.31) | copy-start | bytes 6148
  887.7 41.1 %copy-start.55 = (f32[2,256]{1,0:T(2,128)S(1)}, f32[2,256]{1,0:T(2,128)}, u32[]{:S(2)}) copy-start(f32[2,256]{1,0:T(2,128)} %copy-done.52) | copy-start | bytes 6148
  887.7 41.1 %copy-start.69 = (f32[2,256]{1,0:T(2,128)S(1)}, f32[2,256]{1,0:T(2,128)}, u32[]{:S(2)}) copy-start(f32[2,256]{1,0:T(2,128)} %copy-done.66) | copy-start | bytes 6148
  (53 other events, 137.0 us)
Sparse Core Ops, SparseCore 0:
  11.8 29.8 all-gather.16
  43.8 27.2 all-gather.14
  73.2 27.1 all-gather.12
  102.4 27.1 all-gather.10
  220.2 26.0 reduce-scatter.8
  251.5 26.4 reduce-scatter.4
  280.2 26.0 reduce-scatter.10
  308.7 26.0 reduce-scatter.6
  868.6 52.1 all-gather.18
  924.1 52.9 all-gather.20
  980.5 52.9 all-gather.22
  1036.2 52.9 all-gather.24
  1092.6 62.5 all-gather.26
  1158.4 62.3 all-gather.28
where the time goes:
time: 1250 us; the launch traced here: 1240 us
  blocking collectives  495 us (40%)
  waiting for transfers between devices  323 us (26%)
  matrix products  220 us (18%)
  local copies, waits for them, and re-layouts  118 us (9%)
  other arithmetic  63.5 us (5%)
  between operations  15.5 us (1%)
    unnamed x2, blocking collectives  495 us
    all_gather x6, waiting for transfers between devices, gather_terms(): lax.all_gather(shortened(shares), ('blk', 'dp'), axis=0, tiled=True)  265 us
    dot_general x12, matrix products, back_mul(): jnp.einsum('rne,de->rnd', left, right, preferred_element_type=jnp.float32)  51.4 us
    dot_general x12, matrix products, matmul(): jnp.einsum('rnd,de->rne', left, right, preferred_element_type=jnp.float32)  47.3 us
    dot_general x12, matrix products, outer_sum(): jnp.einsum('rnd,rne->de', left, right, preferred_element_type=jnp.float32)  35.6 us
    convert_element_type x1, other arithmetic, layer_pass(): act = jax.nn.gelu(inner, approximate=False).astype(jnp.bfloat16)  32.8 us
    all_gather x2, waiting for transfers between devices, layer_pass(): lax.all_gather(value, 'blk', axis=1, tiled=True)  30.4 us
    unnamed x232, local copies, waits for them, and re-layouts  28.9 us
  transfers between devices with their start and end apart: 14, of which 9 were waited for; matrix products, arithmetic and copies ran while one was open for 22% of the time, Pallas kernels for 0%

commit v1 on v0

v1 whole, which is shorter than its diff:
```python
import functools
import jax
import jax.numpy as jnp
from jax import lax
from jax.experimental import pallas as pl
from jax.experimental.pallas import tpu as pltpu
from jax.sharding import PartitionSpec as P

HEADS = 12
EPS = 1e-05
F32 = jnp.float32
BF16 = jnp.bfloat16
PAIR = 128
VMEM = 56 * 1024 * 1024
ROOT_HALF = 0.7071067811865476
ROOT_TWO_PI = 0.3989422804014327


def params(steps):
    return pltpu.CompilerParams(
        dimension_semantics=("arbitrary",) * steps, vmem_limit_bytes=VMEM
    )


def dot(left, right):
    return lax.dot_general(left, right, (((1,), (0,)), ((), ())), preferred_element_type=F32)


def dot_nt(left, right):
    return lax.dot_general(left, right, (((1,), (1,)), ((), ())), preferred_element_type=F32)


def dot_tn(left, right):
    return lax.dot_general(left, right, (((0,), (0,)), ((), ())), preferred_element_type=F32)


def normalize(values):
    center = values - jnp.mean(values, axis=-1, keepdims=True)
    scale = lax.rsqrt(jnp.mean(center * center, axis=-1, keepdims=True) + EPS)
    return center * scale, scale


def norm_back(grad, unit, scale, gain):
    scaled = grad * gain
    return scale * (
        scaled
        - jnp.mean(scaled, axis=-1, keepdims=True)
        - unit * jnp.mean(scaled * unit, axis=-1, keepdims=True)
    )


def column_sum(values):
    return jnp.sum(values, axis=0, keepdims=True)


def qkv_kernel(x_ref, gain, shift, wq, wk, wv, bq, bv, first_ref, q_ref, k_ref, v_ref):
    unit, _ = normalize(x_ref[...].astype(F32))
    first = (unit * gain[...] + shift[...]).astype(BF16)
    first_ref[...] = first
    q_ref[...] = ((dot(first, wq[...]) + bq[...]).astype(BF16).astype(F32) * 0.125).astype(BF16)
    k_ref[...] = dot(first, wk[...]).astype(BF16)
    v_ref[...] = (dot(first, wv[...]) + bv[...]).astype(BF16)


def qkv_call(x, gain, shift, wq, wk, wv, bq, bv, tile=256):
    tokens, width = x.shape
    tile_spec = pl.BlockSpec((tile, width), lambda i: (i, 0))
    vec = pl.BlockSpec((1, width), lambda i: (0, 0))
    mat = pl.BlockSpec((width, width), lambda i: (0, 0))
    out = jax.ShapeDtypeStruct((tokens, width), BF16)
    return pl.pallas_call(
        qkv_kernel,
        grid=(tokens // tile,),
        in_specs=[tile_spec, vec, vec, mat, mat, mat, vec, vec],
        out_specs=[tile_spec] * 4,
        out_shape=[out] * 4,
        compiler_params=params(1),
        cost_estimate=pl.CostEstimate(
            flops=6 * tokens * width * width, bytes_accessed=10 * tokens * width, transcendentals=0
        ),
        name="qkv",
    )(x, gain, shift, wq, wk, wv, bq, bv)


def head_masks():
    lane = lax.broadcasted_iota(jnp.int32, (1, PAIR), 1)
    low = (lane < PAIR // 2).astype(F32)
    return low, 1.0 - low


def masked(values, mask):
    return (values.astype(F32) * mask).astype(BF16)


def attention_kernel(q_ref, k_ref, v_ref, mixed_ref, probs_ref):
    length = 2 * q_ref.shape[2]
    q = q_ref[...].reshape(length, PAIR)
    k = k_ref[...].reshape(length, PAIR)
    v = v_ref[...].reshape(length, PAIR)
    total = None
    for head, mask in enumerate(head_masks()):
        scores = dot_nt(masked(q, mask), k)
        weights = jnp.exp(scores - jnp.max(scores, axis=-1, keepdims=True))
        probs = (weights * (1.0 / jnp.sum(weights, axis=-1, keepdims=True))).astype(BF16)
        probs_ref[0, head] = probs
        part = dot(probs, masked(v, mask))
        total = part if total is None else total + part
    mixed_ref[...] = total.astype(BF16).reshape(mixed_ref.shape)


def attention_call(q, k, v):
    halves, rows, half, width = q.shape
    pairs = width // PAIR
    length = 2 * half
    spec = pl.BlockSpec((2, 1, half, PAIR), lambda r, p: (0, r, 0, p))
    return pl.pallas_call(
        attention_kernel,
        grid=(rows, pairs),
        in_specs=[spec] * 3,
        out_specs=[
            spec,
            pl.BlockSpec((1, 2, length, length), lambda r, p: (r * pairs + p, 0, 0, 0)),
        ],
        out_shape=[
            jax.ShapeDtypeStruct(q.shape, BF16),
            jax.ShapeDtypeStruct((rows * pairs, 2, length, length), BF16),
        ],
        compiler_params=params(2),
        cost_estimate=pl.CostEstimate(
            flops=16 * rows * length * length * width,
            bytes_accessed=8 * rows * length * width + 4 * rows * pairs * length * length,
            transcendentals=rows * 2 * pairs * length * length,
        ),
        name="attention",
    )(q, k, v)


def attention_back_kernel(q_ref, k_ref, v_ref, mixed_ref, grad_ref, probs_ref, dq_ref, dk_ref, dv_ref):
    length = 2 * q_ref.shape[2]
    q = q_ref[...].reshape(length, PAIR)
    k = k_ref[...].reshape(length, PAIR)
    v = v_ref[...].reshape(length, PAIR)
    grad = grad_ref[...].reshape(length, PAIR)
    mixed = mixed_ref[...].reshape(length, PAIR)
    dots = grad.astype(F32) * mixed.astype(F32)
    dq = dk = dv = None
    for head, mask in enumerate(head_masks()):
        own = masked(grad, mask)
        probs = probs_ref[0, head]
        grad_probs = dot_nt(own, v)
        delta = jnp.sum(dots * mask, axis=-1, keepdims=True)
        scores = (probs.astype(F32) * (grad_probs - delta)).astype(BF16)
        part_v = dot_tn(probs, own)
        part_q = dot(scores, masked(k, mask))
        part_k = dot_tn(scores, masked(q, mask))
        dq = part_q if dq is None else dq + part_q
        dk = part_k if dk is None else dk + part_k
        dv = part_v if dv is None else dv + part_v
    dq_ref[...] = (dq * 0.125).astype(BF16).reshape(dq_ref.shape)
    dk_ref[...] = dk.astype(BF16).reshape(dk_ref.shape)
    dv_ref[...] = dv.astype(BF16).reshape(dv_ref.shape)


def attention_back_call(q, k, v, mixed, grad, probs):
    halves, rows, half, width = q.shape
    pairs = width // PAIR
    length = 2 * half
    spec = pl.BlockSpec((2, 1, half, PAIR), lambda r, p: (0, r, 0, p))
    return pl.pallas_call(
        attention_back_kernel,
        grid=(rows, pairs),
        in_specs=[spec] * 5
        + [pl.BlockSpec((1, 2, length, length), lambda r, p: (r * pairs + p, 0, 0, 0))],
        out_specs=[spec] * 3,
        out_shape=[jax.ShapeDtypeStruct(q.shape, BF16)] * 3,
        compiler_params=params(2),
        cost_estimate=pl.CostEstimate(
            flops=32 * rows * length * length * width,
            bytes_accessed=16 * rows * length * width + 4 * rows * pairs * length * length,
            transcendentals=0,
        ),
        name="attention_back",
    )(q, k, v, mixed, grad, probs)


def proj_kernel(mixed_ref, x_ref, w, b, gain, shift, resid_ref, second_ref):
    resid = x_ref[...].astype(F32) + (dot(mixed_ref[...], w[...]) + b[...])
    resid_ref[...] = resid
    unit, _ = normalize(resid)
    second_ref[...] = (unit * gain[...] + shift[...]).astype(BF16)


def proj_call(mixed, x, w, b, gain, shift, tile=256):
    tokens, width = x.shape
    tile_spec = pl.BlockSpec((tile, width), lambda i: (i, 0))
    vec = pl.BlockSpec((1, width), lambda i: (0, 0))
    mat = pl.BlockSpec((width, width), lambda i: (0, 0))
    return pl.pallas_call(
        proj_kernel,
        grid=(tokens // tile,),
        in_specs=[tile_spec, tile_spec, mat, vec, vec, vec],
        out_specs=[tile_spec] * 2,
        out_shape=[
            jax.ShapeDtypeStruct((tokens, width), F32),
            jax.ShapeDtypeStruct((tokens, width), BF16),
        ],
        compiler_params=params(1),
        cost_estimate=pl.CostEstimate(
            flops=2 * tokens * width * width, bytes_accessed=10 * tokens * width, transcendentals=0
        ),
        name="proj",
    )(mixed, x, w, b, gain, shift)


def ffn_kernel(tile, start, last, second_ref, grad_ref, w_in, b_in, w_out, base_ref, more_ref, b_out,
               out_ref, gs_ref, dw_ref, dbias_ref, acc, gacc, din_acc, dout_acc):
    step = pl.program_id(0)
    steps = pl.num_programs(0)
    tokens = second_ref.shape[0]

    @pl.when(step == 0)
    def _():
        acc[...] = base_ref[...]
        if start:
            gacc[...] = jnp.zeros_like(gacc)
        else:
            gacc[...] = more_ref[...]

    def body(i, total):
        rows = pl.ds(pl.multiple_of(i * tile, tile), tile)
        second = second_ref[rows, :]
        grad = grad_ref[rows, :]
        inner = dot(second, w_in[...]) + b_in[...]
        dact = dot_nt(grad, w_out[...])
        phi = 0.5 * (1.0 + lax.erf(inner * ROOT_HALF))
        act = (inner * phi).astype(BF16)
        slope = phi + inner * jnp.exp(-0.5 * inner * inner) * ROOT_TWO_PI
        ginner = (dact * slope).astype(BF16)
        acc[rows, :] += dot(act, w_out[...])
        gacc[rows, :] += dot_nt(ginner, w_in[...])
        part_out = dot_tn(act, grad)
        part_in = dot_tn(second, ginner)

        @pl.when(i == 0)
        def _():
            dout_acc[...] = part_out
            din_acc[...] = part_in

        @pl.when(i > 0)
        def _():
            dout_acc[...] += part_out
            din_acc[...] += part_in

        return total + column_sum(ginner.astype(F32))

    total = lax.fori_loop(0, tokens // tile, body, jnp.zeros((1, w_in.shape[1]), F32))
    dbias_ref[...] = total
    dw_ref[0, 0] = din_acc[...].astype(BF16)
    dw_ref[0, 1] = dout_acc[...].astype(BF16)

    @pl.when(step == steps - 1)
    def _():
        if last:
            out_ref[...] = (acc[...] + b_out[...]).astype(BF16)
        else:
            out_ref[...] = acc[...]
        gs_ref[...] = gacc[...]


def ffn_call(second, grad, w_in, b_in, w_out, base, more, b_out, lower, upper, chunk, start, last, tile=512):
    tokens, width = second.shape
    steps = (upper - lower) // chunk
    skip = lower // chunk
    whole = pl.BlockSpec((tokens, width), lambda j: (0, 0))
    vec = pl.BlockSpec((1, width), lambda j: (0, 0))
    more_spec = vec if start else whole
    return pl.pallas_call(
        functools.partial(ffn_kernel, tile, start, last),
        grid=(steps,),
        in_specs=[
            whole,
            whole,
            pl.BlockSpec((width, chunk), lambda j: (0, j + skip)),
            pl.BlockSpec((1, chunk), lambda j: (0, j + skip)),
            pl.BlockSpec((chunk, width), lambda j: (j + skip, 0)),
            whole,
            more_spec,
            vec,
        ],
        out_specs=[
            whole,
            whole,
            pl.BlockSpec((1, 2, width, chunk), lambda j: (j, 0, 0, 0)),
            pl.BlockSpec((1, chunk), lambda j: (0, j)),
        ],
        out_shape=[
            jax.ShapeDtypeStruct((tokens, width), BF16 if last else F32),
            jax.ShapeDtypeStruct((tokens, width), F32),
            jax.ShapeDtypeStruct((steps, 2, width, chunk), BF16),
            jax.ShapeDtypeStruct((1, upper - lower), F32),
        ],
        scratch_shapes=[
            pltpu.VMEM((tokens, width), F32),
            pltpu.VMEM((tokens, width), F32),
            pltpu.VMEM((width, chunk), F32),
            pltpu.VMEM((chunk, width), F32),
        ],
        compiler_params=params(1),
        cost_estimate=pl.CostEstimate(
            flops=12 * tokens * width * (upper - lower),
            bytes_accessed=20 * tokens * width + 8 * width * (upper - lower),
            transcendentals=2 * tokens * (upper - lower),
        ),
        name="ffn",
    )(second, grad, w_in, b_in, w_out, base, more, b_out)


def proj_back_kernel(gs_ref, resid_ref, grad_ref, mixed_ref, w, gain,
                     gresid_ref, gmixed_ref, dw_ref, vec_ref, dw_acc, vec_acc):
    step = pl.program_id(0)
    steps = pl.num_programs(0)
    unit, scale = normalize(resid_ref[...])
    gs = gs_ref[...]
    grad = grad_ref[...].astype(F32)
    gresid = grad + norm_back(gs, unit, scale, gain[...])
    gresid_ref[...] = gresid
    branch = gresid.astype(BF16)
    gmixed_ref[...] = dot_nt(branch, w[...]).astype(BF16)
    part = dot_tn(mixed_ref[...], branch)
    sums = jnp.concatenate(
        [
            column_sum(gs * unit),
            column_sum(gs),
            column_sum(branch.astype(F32)),
            column_sum(grad),
            jnp.zeros((4, gs.shape[1]), F32),
        ],
        axis=0,
    )

    @pl.when(step == 0)
    def _():
        dw_acc[...] = part
        vec_acc[...] = sums

    @pl.when(step > 0)
    def _():
        dw_acc[...] += part
        vec_acc[...] += sums

    @pl.when(step == steps - 1)
    def _():
        dw_ref[...] = dw_acc[...].astype(BF16)
        vec_ref[...] = vec_acc[...]


def proj_back_call(gs, resid, grad, mixed, w, gain, tile=256):
    tokens, width = resid.shape
    tile_spec = pl.BlockSpec((tile, width), lambda i: (i, 0))
    vec = pl.BlockSpec((1, width), lambda i: (0, 0))
    mat = pl.BlockSpec((width, width), lambda i: (0, 0))
    return pl.pallas_call(
        proj_back_kernel,
        grid=(tokens // tile,),
        in_specs=[tile_spec] * 4 + [mat, vec],
        out_specs=[tile_spec, tile_spec, mat, pl.BlockSpec((8, width), lambda i: (0, 0))],
        out_shape=[
            jax.ShapeDtypeStruct((tokens, width), F32),
            jax.ShapeDtypeStruct((tokens, width), BF16),
            jax.ShapeDtypeStruct((width, width), BF16),
            jax.ShapeDtypeStruct((8, width), F32),
        ],
        scratch_shapes=[pltpu.VMEM((width, width), F32), pltpu.VMEM((8, width), F32)],
        compiler_params=params(1),
        cost_estimate=pl.CostEstimate(
            flops=4 * tokens * width * width, bytes_accessed=18 * tokens * width, transcendentals=0
        ),
        name="proj_back",
    )(gs, resid, grad, mixed, w, gain)


def qkv_back_kernel(dq_ref, dk_ref, dv_ref, first_ref, x_ref, gresid_ref, wq, wk, wv, gain,
                    gin_ref, dw_ref, vec_ref, dw_acc, vec_acc):
    step = pl.program_id(0)
    steps = pl.num_programs(0)
    dq, dk, dv, first = dq_ref[...], dk_ref[...], dv_ref[...], first_ref[...]
    gfirst = dot_nt(dq, wq[...]) + dot_nt(dk, wk[...]) + dot_nt(dv, wv[...])
    unit, scale = normalize(x_ref[...].astype(F32))
    gin_ref[...] = (gresid_ref[...] + norm_back(gfirst, unit, scale, gain[...])).astype(BF16)
    parts = [dot_tn(first, part) for part in (dq, dk, dv)]
    sums = jnp.concatenate(
        [
            column_sum(gfirst * unit),
            column_sum(gfirst),
            column_sum(dq.astype(F32)),
            column_sum(dv.astype(F32)),
            jnp.zeros((4, first.shape[1]), F32),
        ],
        axis=0,
    )

    @pl.when(step == 0)
    def _():
        for n, part in enumerate(parts):
            dw_acc[n] = part
        vec_acc[...] = sums

    @pl.when(step > 0)
    def _():
        for n, part in enumerate(parts):
            dw_acc[n] += part
        vec_acc[...] += sums

    @pl.when(step == steps - 1)
    def _():
        dw_ref[...] = dw_acc[...].astype(BF16)
        vec_ref[...] = vec_acc[...]


def qkv_back_call(dq, dk, dv, first, x, gresid, wq, wk, wv, gain, tile=256):
    tokens, width = x.shape
    tile_spec = pl.BlockSpec((tile, width), lambda i: (i, 0))
    vec = pl.BlockSpec((1, width), lambda i: (0, 0))
    mat = pl.BlockSpec((width, width), lambda i: (0, 0))
    return pl.pallas_call(
        qkv_back_kernel,
        grid=(tokens // tile,),
        in_specs=[tile_spec] * 6 + [mat] * 3 + [vec],
        out_specs=[
            tile_spec,
            pl.BlockSpec((3, width, width), lambda i: (0, 0, 0)),
            pl.BlockSpec((8, width), lambda i: (0, 0)),
        ],
        out_shape=[
            jax.ShapeDtypeStruct((tokens, width), BF16),
            jax.ShapeDtypeStruct((3, width, width), BF16),
            jax.ShapeDtypeStruct((8, width), F32),
        ],
        scratch_shapes=[pltpu.VMEM((3, width, width), F32), pltpu.VMEM((8, width), F32)],
        compiler_params=params(1),
        cost_estimate=pl.CostEstimate(
            flops=12 * tokens * width * width, bytes_accessed=20 * tokens * width, transcendentals=0
        ),
        name="qkv_back",
    )(dq, dk, dv, first, x, gresid, wq, wk, wv, gain)


def swap(values, hop):
    axis, bit, size = hop
    pairs = [(i, i ^ bit) for i in range(size)]
    return lax.ppermute(values, axis, pairs)


def side_of(hop):
    axis, bit, _ = hop
    return (lax.axis_index(axis) // bit) % 2


def reduce_hop(values, hop):
    half = values.shape[0] // 2
    side = side_of(hop)
    kept = lax.dynamic_slice_in_dim(values, side * half, half, 0)
    sent = lax.dynamic_slice_in_dim(values, (1 - side) * half, half, 0)
    return (kept.astype(F32) + swap(sent, hop).astype(F32)).astype(BF16)


def gather_hop(values, hop):
    other = swap(values, hop)
    side = side_of(hop)
    return jnp.concatenate(
        [jnp.where(side == 0, values, other), jnp.where(side == 0, other, values)], axis=0
    )


def sum_over_devices(values, hops):
    for hop in hops:
        values = reduce_hop(values, hop)
    for hop in reversed(hops):
        values = gather_hop(values, hop)
    return values


def on_device(
    sizes,
    inputs,
    cotangent,
    flags,
    gain_one,
    shift_one,
    query_weight,
    query_bias,
    key_weight,
    value_weight,
    value_bias,
    proj_weight,
    proj_bias,
    gain_two,
    shift_two,
    inner_weight,
    inner_bias,
    outer_weight,
    outer_bias,
):
    batch, half, width = inputs.shape
    hidden = inner_weight.shape[1]
    rows = batch // 2
    blk_hop = ("blk", 1, sizes["blk"])
    bits = [1 << n for n in range(sizes["dp"].bit_length() - 1)]
    dp_hops = [("dp", bit, sizes["dp"]) for bit in bits]
    hops = dp_hops[:2] + [blk_hop] + dp_hops[2:]

    def row(vector):
        return vector.reshape(1, -1)

    masked_flags = jnp.max(flags.reshape(batch, half, -1), axis=-1)
    grad_low = jnp.where(masked_flags[:, :, None] > 0, cotangent, jnp.zeros_like(cotangent))
    mine = lax.axis_index("blk") * rows
    theirs = (1 - lax.axis_index("blk")) * rows

    def both_halves(values):
        kept = lax.dynamic_slice_in_dim(values, mine, rows, 0)
        sent = lax.dynamic_slice_in_dim(values, theirs, rows, 0)
        return jnp.concatenate([kept, swap(sent, blk_hop)], axis=0).reshape(batch * half, width)

    def home(values):
        values = values.reshape(2, rows, half, width)
        back = swap(values[1], blk_hop)
        side = side_of(blk_hop)
        return jnp.concatenate(
            [jnp.where(side == 0, values[0], back), jnp.where(side == 0, back, values[0])], axis=0
        )

    x = both_halves(inputs)
    grad = both_halves(grad_low)
    first, q, k, v = qkv_call(
        x, row(gain_one), row(shift_one), query_weight, key_weight, value_weight,
        row(query_bias), row(value_bias),
    )
    grouped = (2, rows, half, width)
    q, k, v = (t.reshape(grouped) for t in (q, k, v))
    mixed, probs = attention_call(q, k, v)
    mixed_flat = mixed.reshape(x.shape)
    resid, second = proj_call(
        mixed_flat, x, proj_weight, row(proj_bias), row(gain_two), row(shift_two)
    )
    middle = hidden // 2
    chunk = width
    out_part, gs_part, blocks_one, bias_one = ffn_call(
        second, grad, inner_weight, row(inner_bias), outer_weight, resid, row(gain_one),
        row(outer_bias), 0, middle, chunk, True, False,
    )
    out, gs, blocks_two, bias_two = ffn_call(
        second, grad, inner_weight, row(inner_bias), outer_weight, out_part, gs_part,
        row(outer_bias), middle, hidden, chunk, False, True,
    )
    gresid, gmixed, dw_proj, vec_two = proj_back_call(
        gs, resid, grad, mixed_flat, proj_weight, row(gain_two)
    )
    dq, dk, dv = attention_back_call(q, k, v, mixed, gmixed.reshape(grouped), probs)
    dq, dk, dv = (t.reshape(x.shape) for t in (dq, dk, dv))
    gin, dw_qkv, vec_one = qkv_back_call(
        dq, dk, dv, first, x, gresid, query_weight, key_weight, value_weight, row(gain_one)
    )
    output = home(out)
    input_grad = home(gin)

    vectors = jnp.concatenate(
        [vec_one[0:4].reshape(-1), vec_two[0:4].reshape(-1), bias_one.reshape(-1), bias_two.reshape(-1)]
    )
    vectors = lax.psum(vectors, ("blk", "dp"))
    gain_one_grad, shift_one_grad, query_bias_grad, value_bias_grad = (
        vectors[n * width : (n + 1) * width] for n in range(4)
    )
    gain_two_grad, shift_two_grad, proj_bias_grad, outer_bias_grad = (
        vectors[n * width : (n + 1) * width] for n in range(4, 8)
    )
    inner_bias_grad = vectors[8 * width :]

    def square(values):
        return values.reshape(-1, width, width)

    one = square(sum_over_devices(blocks_one.reshape(-1, width), hops))
    two = square(sum_over_devices(blocks_two.reshape(-1, width), hops))
    rest = jnp.concatenate([dw_proj, dw_qkv.reshape(-1, width)], axis=0)
    rest = square(sum_over_devices(rest, hops)).astype(F32)
    steps = middle // chunk
    inner_weight_grad = jnp.concatenate(
        [one[2 * n] for n in range(steps)] + [two[2 * n] for n in range(steps)], axis=1
    ).astype(F32)
    outer_weight_grad = jnp.concatenate(
        [one[2 * n + 1] for n in range(steps)] + [two[2 * n + 1] for n in range(steps)], axis=0
    ).astype(F32)
    return (
        output,
        input_grad,
        gain_one_grad,
        shift_one_grad,
        rest[1],
        query_bias_grad,
        rest[2],
        rest[3],
        value_bias_grad,
        rest[0],
        proj_bias_grad,
        gain_two_grad,
        shift_two_grad,
        inner_weight_grad,
        inner_bias_grad,
        outer_weight_grad,
        outer_bias_grad,
    )


def solution(mesh):
    sizes = dict(mesh.shape)
    split = P("dp", "blk", None)
    in_specs = (split, split, P("dp", "blk")) + (P(),) * 15
    out_specs = (split, split) + (P(),) * 15
    return jax.shard_map(
        functools.partial(on_device, sizes),
        mesh=mesh,
        in_specs=in_specs,
        out_specs=out_specs,
        check_vma=False,
    )
```

time: 1250 us -> 490 us (0.39)
  blocking collectives: 495 us -> 99.8 us
  matrix products: 220 us -> 0 us
  waiting for transfers between devices: 323 us -> 128 us
  Pallas kernels: 0 us -> 139 us
  local copies, waits for them, and re-layouts: 118 us -> 24.8 us
  starting transfers between devices: 1.37 us -> 43 us
  other arithmetic: 63.5 us -> 44.5 us
  between operations: 15.5 us -> 1.92 us
    unnamed x2 -> x0, blocking collectives: 495 us -> none
    all_gather x10 -> x0, waiting for transfers between devices: 323 us -> none  [the longest x6 265 us: gather_terms(): lax.all_gather(shortened(shares), ('blk', 'dp'), axis=0, tiled=True)]
    dot_general x46 -> x0, matrix products: 199 us -> none  [the longest x12 51.4 us: back_mul(): jnp.einsum('rne,de->rnd', left, right, preferred_element_type=jnp.float32)]
    pallas_call x0 -> x8, Pallas kernels: none -> 139 us  [the longest x2 53.3 us: ffn_call(): pl.pallas_call(functools.partial(ffn_kernel, tile, start, last), grid=(st...]
    ppermute x0 -> x34, waiting for transfers between devices: none -> 128 us  [swap(): return lax.ppermute(values, axis, pairs)]
    psum x0 -> x1, blocking collectives: none -> 99.8 us  [on_device(): vectors = lax.psum(vectors, ('blk', 'dp'))]
    ppermute x0 -> x34, starting transfers between devices: none -> 43 us  [swap(): return lax.ppermute(values, axis, pairs)]
    reshape x7 -> x11, local copies, waits for them, and re-layouts: 33.5 us -> 5.2 us  [the longest x8 4.64 us: row(): return vector.reshape(1, -1)]
  transfers between devices with their start and end apart: 14 -> 34, of which waited for: 9 -> 15; matrix products, arithmetic and copies ran while one was open for 22% -> 10% of each run, Pallas kernels for 0% -> 7%
where the time goes in v1:
time: 490 us; the launch traced here: 481 us
  Pallas kernels  139 us (28%)
  waiting for transfers between devices  128 us (26%)
  blocking collectives  99.8 us (20%)
  other arithmetic  44.5 us (9%)
  starting transfers between devices  43 us (9%)
  local copies, waits for them, and re-layouts  24.8 us (5%)
    ppermute x34, waiting for transfers between devices, swap(): return lax.ppermute(values, axis, pairs)  128 us
    psum x1, blocking collectives, on_device(): vectors = lax.psum(vectors, ('blk', 'dp'))  99.8 us
    pallas_call x2, Pallas kernels, ffn_call(): pl.pallas_call(functools.partial(ffn_kernel, tile, start, last), grid=(st...  53.3 us
    ppermute x34, starting transfers between devices, swap(): return lax.ppermute(values, axis, pairs)  43 us
    pallas_call x1, Pallas kernels, attention_back_call(): pl.pallas_call(attention_back_kernel, grid=(rows, pairs), in_specs=[spec]...  22.9 us
    pallas_call x1, Pallas kernels, attention_call(): pl.pallas_call(attention_kernel, grid=(rows, pairs), in_specs=[spec] * 3,...  21.1 us
    pallas_call x1, Pallas kernels, qkv_back_call(): pl.pallas_call(qkv_back_kernel, grid=(tokens // tile,), in_specs=[tile_sp...  17 us
    convert_element_type x15, other arithmetic, reduce_hop(): return (kept.astype(F32) + swap(sent, hop).astype(F32)).astype(BF16)  14.9 us
  transfers between devices with their start and end apart: 34, of which 15 were waited for; matrix products, arithmetic and copies ran while one was open for 10% of the time, Pallas kernels for 7%

profile of v1, /device:TPU:0, one launch (start us, length us, event | category | flops | bytes accessed | tf_op | source)
XLA Modules:
  0.0 481.3 jit_solution(4957211789631588825)
XLA Ops:
  0.7 2.5 constant_dynamic-slice_fusion.17
  3.2 3.0 collective-permute-start
  12.5 12.3 %collective-permute-done = bf16[2,256,768]{2,1,0:T(8,128)(2,1)} collective-permute-done((bf16[2,256,768]{2,1,0:T(8,128)(2,1)}, bf16[2,256,768]{2,1,0:T(8,128)(2,1)}, u32[]{:S(2)}, u32[]{:S(2)}) %collective-permute-start) | collective-permute-done | bytes 786464 | tf_op jit(solution)/shard_map/ppermute | solution.py:451
  24.8 2.4 pad_maximum_fusion.3
  27.2 8.2 %qkv.1 = (bf16[1024,768]{1,0:T(8,128)(2,1)}, bf16[1024,768]{1,0:T(8,128)(2,1)}, bf16[1024,768]{1,0:T(8,128)(2,1)}, bf16[1024,768]{1,0:T(8,128)(2,1)}) custom-call(bf16[1024,768]{1,0:T(8,128)(2,1)} %bitcast.35, f32[1,768]{1,0:T(1,128)} %reshape.163.gain.more_ref, f32[1,768]{1,0:T(1,128)} %reshape.164.shift, bf16[768,768]{1,0:T(8,128)(2,1)} %wq.3, ...), custom_call_target="tpu_custom_call" | custom-call | flops 3623878656 | bytes 7864320 | tf_op jit(solution)/shard_map/qkv/pallas_call | solution.py:71
  35.5 21.1 %attention.1 = (bf16[2,2,256,768]{3,2,1,0:T(8,128)(2,1)}, bf16[12,2,512,512]{3,2,1,0:T(8,128)(2,1)}) custom-call(bf16[2,2,256,768]{3,2,1,0:T(8,128)(2,1)} %bitcast.42, bf16[2,2,256,768]{3,2,1,0:T(8,128)(2,1)} %bitcast.44, bf16[2,2,256,768]{3,2,1,0:T(8,128)(2,1)} %bitcast.46), custom_call_target="tpu_custom_call" | custom-call | flops 6442450944 | bytes 18874368 | tf_op jit(solution)/shard_map/attention/pallas_call | solution.py:116
  56.5 5.9 %proj.1 = (f32[1024,768]{1,0:T(8,128)}, bf16[1024,768]{1,0:T(8,128)(2,1)}) custom-call(bf16[1024,768]{1,0:T(8,128)(2,1)} %bitcast.33, bf16[1024,768]{1,0:T(8,128)(2,1)} %bitcast.36, bf16[768,768]{1,0:T(8,128)(2,1)} %w.3, f32[1,768]{1,0:T(1,128)} %reshape.171.b, f32[1,768]{1,0:T(1,128)} %reshape.172.gain, f32[1,768]{1,0:T(1,128)} %reshape.173.shift), custom_call_target="tpu_custom_call" | custom-call | flops 1207959552 | bytes 7864320 | tf_op jit(solution)/shard_map/proj/pallas_call | solution.py:198
  62.5 1.3 pad_maximum_fusion.4
  63.8 26.4 %ffn.2 = (f32[1024,768]{1,0:T(8,128)}, f32[1024,768]{1,0:T(8,128)}, bf16[2,2,768,768]{3,2,1,0:T(8,128)(2,1)}, f32[1,1536]{1,0:T(1,128)}) custom-call(bf16[1024,768]{1,0:T(8,128)(2,1)} %get-tuple-element.47.second_ref, bf16[1024,768]{1,0:T(8,128)(2,1)} %bitcast.20, bf16[768,3072]{1,0:T(8,128)(2,1)} %w_in.3, f32[1,3072]{1,0:T(1,128)} %bitcast.40, ...), custom_call_target="tpu_custom_call" | custom-call | flops 14495514624 | bytes 25165824 | tf_op jit(solution)/shard_map/ffn/pallas_call | solution.py:277
  90.1 26.9 %ffn.3 = (bf16[1024,768]{1,0:T(8,128)(2,1)}, f32[1024,768]{1,0:T(8,128)}, bf16[2,2,768,768]{3,2,1,0:T(8,128)(2,1)}, f32[1,1536]{1,0:T(1,128)}) custom-call(bf16[1024,768]{1,0:T(8,128)(2,1)} %get-tuple-element.47.second_ref, bf16[1024,768]{1,0:T(8,128)(2,1)} %bitcast.21, bf16[768,3072]{1,0:T(8,128)(2,1)} %w_in.3, f32[1,3072]{1,0:T(1,128)} %bitcast.41, ...), custom_call_target="tpu_custom_call" | custom-call | flops 14495514624 | bytes 25165824 | tf_op jit(solution)/shard_map/ffn/pallas_call | solution.py:277
  117.0 10.6 %proj_back.1 = (f32[1024,768]{1,0:T(8,128)}, bf16[1024,768]{1,0:T(8,128)(2,1)}, bf16[768,768]{1,0:T(8,128)(2,1)}, f32[8,768]{1,0:T(8,128)}) custom-call(f32[1024,768]{1,0:T(8,128)} %get-tuple-element.52.gs_ref, f32[1024,768]{1,0:T(8,128)} %get-tuple-element.48.base_ref.resid_ref, bf16[1024,768]{1,0:T(8,128)(2,1)} %bitcast.22, bf16[1024,768]{1,0:T(8,128)(2,1)} %bitcast.34, ...), custom_call_target="tpu_custom_call" | custom-call | flops 2415919104 | bytes 14155776 | tf_op jit(solution)/shard_map/proj_back/pallas_call | solution.py:362
  127.6 22.9 %attention_back.1 = (bf16[2,2,256,768]{3,2,1,0:T(8,128)(2,1)}, bf16[2,2,256,768]{3,2,1,0:T(8,128)(2,1)}, bf16[2,2,256,768]{3,2,1,0:T(8,128)(2,1)}) custom-call(bf16[2,2,256,768]{3,2,1,0:T(8,128)(2,1)} %bitcast.43, bf16[2,2,256,768]{3,2,1,0:T(8,128)(2,1)} %bitcast.45, bf16[2,2,256,768]{3,2,1,0:T(8,128)(2,1)} %bitcast.47, ...), custom_call_target="tpu_custom_call" | custom-call | flops 12884901888 | bytes 25165824 | tf_op jit(solution)/shard_map/attention_back/pallas_call | solution.py:169
  150.5 17.0 %qkv_back.1 = (bf16[1024,768]{1,0:T(8,128)(2,1)}, bf16[3,768,768]{2,1,0:T(8,128)(2,1)}, f32[8,768]{1,0:T(8,128)}) custom-call(bf16[1024,768]{1,0:T(8,128)(2,1)} %bitcast.48, bf16[1024,768]{1,0:T(8,128)(2,1)} %bitcast.49, bf16[1024,768]{1,0:T(8,128)(2,1)} %bitcast.50, bf16[1024,768]{1,0:T(8,128)(2,1)} %get-tuple-element.58.first_ref, ...), custom_call_target="tpu_custom_call" | custom-call | flops 7247757312 | bytes 15728640 | tf_op jit(solution)/shard_map/qkv_back/pallas_call | solution.py:425
  167.6 4.3 fusion
  171.9 1.6 constant_dynamic-slice_fusion.4
  174.0 3.4 constant_dynamic-slice_fusion.9
  177.4 3.6 add_convert_fusion.2
  181.0 1.1 constant_dynamic-slice_fusion.13
  182.1 2.0 collective-permute-start.5
  184.2 3.0 add_convert_fusion
  187.2 1.2 constant_dynamic-slice_fusion.3
  188.3 1.3 collective-permute-start.25
  189.6 2.3 add_convert_fusion.1
  192.0 1.1 constant_dynamic-slice_fusion.8
  193.8 1.0 fusion.7
  194.8 1.6 collective-permute-start.3
  196.6 99.8 %psum.7 = f32[9216]{0:T(1024)S(1)} all-reduce(f32[9216]{0:T(1024)S(1)} %pad_maximum_fusion.16), channel_id=1, replica_groups=mesh['blk'=2,'dp'=16] {'blk','dp'}, use_global_device_ids=true, to_apply=%region_1.2 | all-reduce | flops 9216 | bytes 73728 | tf_op jit(solution)/shard_map/psum | solution.py:570
  297.0 2.1 add_convert_fusion.5
  299.1 2.3 collective-permute-start.6
  301.5 1.6 add_convert_fusion.3
  303.4 1.6 add_convert_fusion.4
  305.0 1.9 collective-permute-start.16
  306.9 8.8 %collective-permute-done.6 = bf16[384,768]{1,0:T(8,128)(2,1)S(1)} collective-permute-done((bf16[384,768]{1,0:T(8,128)(2,1)S(1)}, bf16[384,768]{1,0:T(8,128)(2,1)S(1)}, u32[]{:S(2)}, u32[]{:S(2)}) %collective-permute-start.6) | collective-permute-done | bytes 589856 | tf_op jit(solution)/shard_map/ppermute | solution.py:451
  316.4 11.9 %collective-permute-done.26 = bf16[384,768]{1,0:T(8,128)(2,1)S(1)} collective-permute-done((bf16[384,768]{1,0:T(8,128)(2,1)S(1)}, bf16[384,768]{1,0:T(8,128)(2,1)S(1)}, u32[]{:S(2)}, u32[]{:S(2)}) %collective-permute-start.26) | collective-permute-done | bytes 589856 | tf_op jit(solution)/shard_map/ppermute | solution.py:451
  329.0 9.7 %collective-permute-done.16 = bf16[384,768]{1,0:T(8,128)(2,1)S(1)} collective-permute-done((bf16[384,768]{1,0:T(8,128)(2,1)S(1)}, bf16[384,768]{1,0:T(8,128)(2,1)S(1)}, u32[]{:S(2)}, u32[]{:S(2)}) %collective-permute-start.16) | collective-permute-done | bytes 589856 | tf_op jit(solution)/shard_map/ppermute | solution.py:451
  339.6 1.7 collective-permute-start.28
  341.4 1.3 collective-permute-start.8
  342.7 7.0 %collective-permute-done.28 = bf16[96,768]{1,0:T(8,128)(2,1)S(1)} collective-permute-done((bf16[96,768]{1,0:T(8,128)(2,1)S(1)}, bf16[96,768]{1,0:T(8,128)(2,1)S(1)}, u32[]{:S(2)}, u32[]{:S(2)}) %collective-permute-start.28) | collective-permute-done | bytes 147488 | tf_op jit(solution)/shard_map/ppermute | solution.py:451
  349.8 3.5 collective-permute-start.29
  353.5 11.0 %collective-permute-done.29 = bf16[96,768]{1,0:T(8,128)(2,1)S(1)} collective-permute-done((bf16[96,768]{1,0:T(8,128)(2,1)S(1)}, bf16[96,768]{1,0:T(8,128)(2,1)S(1)}, u32[]{:S(2)}, u32[]{:S(2)}) %collective-permute-start.29) | collective-permute-done | bytes 147488 | tf_op jit(solution)/shard_map/ppermute | solution.py:451
  364.8 2.8 collective-permute-start.9
  367.6 1.4 collective-permute-done.18
  369.1 6.2 %collective-permute-done.30 = bf16[192,768]{1,0:T(8,128)(2,1)S(1)} collective-permute-done((bf16[192,768]{1,0:T(8,128)(2,1)S(1)}, bf16[192,768]{1,0:T(8,128)(2,1)S(1)}, u32[]{:S(2)}, u32[]{:S(2)}) %collective-permute-start.30) | collective-permute-done | bytes 294944 | tf_op jit(solution)/shard_map/ppermute | solution.py:451
  376.3 1.0 collective-permute-done.9
  377.4 1.4 collective-permute-done.19
  379.6 7.8 %collective-permute-done.31 = bf16[384,768]{1,0:T(8,128)(2,1)S(1)} collective-permute-done((bf16[384,768]{1,0:T(8,128)(2,1)S(1)}, bf16[384,768]{1,0:T(8,128)(2,1)S(1)}, u32[]{:S(2)}, u32[]{:S(2)}) %collective-permute-start.31) | collective-permute-done | bytes 589856 | tf_op jit(solution)/shard_map/ppermute | solution.py:451
  387.7 7.8 %collective-permute-start.32 = (bf16[768,768]{1,0:T(8,128)(2,1)S(1)}, bf16[768,768]{1,0:T(8,128)(2,1)S(1)}, u32[]{:S(2)}, u32[]{:S(2)}) collective-permute-start(bf16[768,768]{1,0:T(8,128)(2,1)S(1)} %pad_maximum_fusion.9), channel_id=1, source_target_pairs={{0,2},{1,3},{2,0},{3,1},{4,6},{5,7},{6,4},{7,5},{8,10},{9,11},{10,... | collective-permute-start | bytes 3538952 | tf_op jit(solution)/shard_map/ppermute | solution.py:451
  396.5 2.1 collective-permute-start.21
  398.6 7.6 %collective-permute-done.11 = bf16[384,768]{1,0:T(8,128)(2,1)S(1)} collective-permute-done((bf16[384,768]{1,0:T(8,128)(2,1)S(1)}, bf16[384,768]{1,0:T(8,128)(2,1)S(1)}, u32[]{:S(2)}, u32[]{:S(2)}) %collective-permute-start.11) | collective-permute-done | bytes 589856 | tf_op jit(solution)/shard_map/ppermute | solution.py:451
  406.5 4.8 collective-permute-start.12
  411.3 11.1 %collective-permute-done.32 = bf16[768,768]{1,0:T(8,128)(2,1)S(1)} collective-permute-done((bf16[768,768]{1,0:T(8,128)(2,1)S(1)}, bf16[768,768]{1,0:T(8,128)(2,1)S(1)}, u32[]{:S(2)}, u32[]{:S(2)}) %collective-permute-start.32) | collective-permute-done | bytes 1179680 | tf_op jit(solution)/shard_map/ppermute | solution.py:451
  423.1 1.2 copy-done.6
  424.8 1.6 collective-permute-start.22
  426.4 19.9 %collective-permute-done.12 = bf16[768,768]{1,0:T(8,128)(2,1)S(1)} collective-permute-done((bf16[768,768]{1,0:T(8,128)(2,1)S(1)}, bf16[768,768]{1,0:T(8,128)(2,1)S(1)}, u32[]{:S(2)}, u32[]{:S(2)}) %collective-permute-start.12) | collective-permute-done | bytes 1179680 | tf_op jit(solution)/shard_map/ppermute | solution.py:451
  446.9 1.3 broadcast_select_fusion.14
  448.3 1.3 pad_maximum_fusion.5
  449.6 1.3 pad_maximum_fusion.6
  450.8 11.0 %collective-permute-done.22 = bf16[768,768]{1,0:T(8,128)(2,1)S(1)} collective-permute-done((bf16[768,768]{1,0:T(8,128)(2,1)S(1)}, bf16[768,768]{1,0:T(8,128)(2,1)S(1)}, u32[]{:S(2)}, u32[]{:S(2)}) %collective-permute-start.22) | collective-permute-done | bytes 1179680 | tf_op jit(solution)/shard_map/ppermute | solution.py:451
  462.5 1.0 broadcast_select_fusion.1
  463.9 1.0 broadcast_select_fusion.5
  465.6 3.8 fusion.2
  469.5 2.7 broadcast_select_fusion.3
  472.5 4.3 maximum_convert_fusion.1
  476.8 4.0 maximum_convert_fusion.2
  (158 shorter events, 18.6 us)
Async XLA Ops:
  0.7 5.5 %copy-start.8 = (s32[4,1024]{1,0:T(4,128)S(1)}, s32[4,1024]{1,0:T(4,128)}, u32[]{:S(2)}) copy-start(s32[4,1024]{1,0:T(4,128)} %param.20) | copy-start | bytes 49156
  0.7 6.2 %copy-start.5 = (bf16[4,256,768]{2,1,0:T(8,128)(2,1)S(1)}, bf16[4,256,768]{2,1,0:T(8,128)(2,1)}, u32[]{:S(2)}) copy-start(bf16[4,256,768]{2,1,0:T(8,128)(2,1)} %param.19) | copy-start | bytes 4718596
  3.2 21.6 %collective-permute-start = (bf16[2,256,768]{2,1,0:T(8,128)(2,1)}, bf16[2,256,768]{2,1,0:T(8,128)(2,1)}, u32[]{:S(2)}, u32[]{:S(2)}) collective-permute-start(bf16[2,256,768]{2,1,0:T(8,128)(2,1)} %get-tuple-element.104), channel_id=1, source_target_pairs={{0,16},{16,0},{1,17},{17,1},{2,18},{18,2},{3,19},{19,3},{4,20},{20... | collective-permute-start | bytes 2359304 | tf_op jit(solution)/shard_map/ppermute | solution.py:451
  7.1 0.7 copy-start.13
  7.1 1.3 copy-start.14
  7.1 1.8 copy-start.15
  7.2 2.4 copy-start.16
  7.2 3.0 copy-start.17
  7.2 3.5 copy-start.18
  7.2 4.1 copy-start.19
  7.2 4.7 copy-start.20
  7.3 55.1 %collective-permute-start.1 = (bf16[2,256,768]{2,1,0:T(8,128)(2,1)S(1)}, bf16[2,256,768]{2,1,0:T(8,128)(2,1)S(1)}, u32[]{:S(2)}, u32[]{:S(2)}) collective-permute-start(bf16[2,256,768]{2,1,0:T(8,128)(2,1)S(1)} %get-tuple-element.102), channel_id=1, source_target_pairs={{0,16},{16,0},{1,17},{17,1},{2,18},{18,2},{3,19},{19,3},{4,20},{20... | collective-permute-start | bytes 2359304 | tf_op jit(solution)/shard_map/ppermute | solution.py:451
  117.0 54.9 %slice-start.2 = ((s8[4718592]{0:T(1024)(128)(4,1)}), s8[4194304]{0:T(1024)(128)(4,1)S(1)}, s32[]{:S(2)}) async-start(s8[4718592]{0:T(1024)(128)(4,1)} %bitcast.28), calls=%async_computation.2 | async-start | bytes 8388608
  127.6 44.3 %slice-start.3 = ((s8[4718592]{0:T(1024)(128)(4,1)}), s8[524288]{0:T(1024)(128)(4,1)S(1)}, s32[]{:S(2)}) async-start(s8[4718592]{0:T(1024)(128)(4,1)} %bitcast.28), calls=%async_computation.3 | async-start | bytes 1048576
  150.5 17.1 %copy-start.4 = (bf16[768,768]{1,0:T(8,128)(2,1)S(1)}, bf16[768,768]{1,0:T(8,128)(2,1)}, u32[]{:S(2)}) copy-start(bf16[768,768]{1,0:T(8,128)(2,1)} %get-tuple-element.65) | copy-start | bytes 3538948
  171.9 5.5 %collective-permute-start.4 = (bf16[1536,768]{1,0:T(8,128)(2,1)}, bf16[1536,768]{1,0:T(8,128)(2,1)}, u32[]{:S(2)}, u32[]{:S(2)}) collective-permute-start(bf16[1536,768]{1,0:T(8,128)(2,1)} %fusion), channel_id=1, source_target_pairs={{0,1},{1,0},{2,3},{3,2},{4,5},{5,4},{6,7},{7,6},{8,9},{9,8},{10,11... | collective-permute-start | bytes 7077896 | tf_op jit(solution)/shard_map/ppermute | solution.py:451
  173.5 10.7 %collective-permute-start.24 = (bf16[1536,768]{1,0:T(8,128)(2,1)}, bf16[1536,768]{1,0:T(8,128)(2,1)}, u32[]{:S(2)}, u32[]{:S(2)}) collective-permute-start(bf16[1536,768]{1,0:T(8,128)(2,1)} %constant_dynamic-slice_fusion.4), channel_id=1, source_target_pairs={{0,1},{1,0},{2,3},{3,2},{4,5},{5,4},{6,7},{7,6},{8,9},{9,8},{10,11... | collective-permute-start | bytes 7077896 | tf_op jit(solution)/shard_map/ppermute | solution.py:451
  174.0 3.4 copy-start
  177.4 12.3 %collective-permute-start.14 = (bf16[1536,768]{1,0:T(8,128)(2,1)}, bf16[1536,768]{1,0:T(8,128)(2,1)}, u32[]{:S(2)}, u32[]{:S(2)}) collective-permute-start(bf16[1536,768]{1,0:T(8,128)(2,1)} %constant_dynamic-slice_fusion.9), channel_id=1, source_target_pairs={{0,1},{1,0},{2,3},{3,2},{4,5},{5,4},{6,7},{7,6},{8,9},{9,8},{10,11... | collective-permute-start | bytes 7077896 | tf_op jit(solution)/shard_map/ppermute | solution.py:451
  181.0 6.1 %copy-start.3 = (bf16[1536,768]{1,0:T(8,128)(2,1)}, bf16[1536,768]{1,0:T(8,128)(2,1)S(1)}, u32[]{:S(2)}) copy-start(bf16[1536,768]{1,0:T(8,128)(2,1)S(1)} %add_convert_fusion.2) | copy-start | bytes 7077892
  181.0 8.6 %slice-start = ((s8[4718592]{0:T(1024)(128)(4,1)}), s8[4194304]{0:T(1024)(128)(4,1)S(1)}, s32[]{:S(2)}) async-start(s8[4718592]{0:T(1024)(128)(4,1)} %bitcast.24), calls=%async_computation | async-start | bytes 8388608
  182.1 7.5 %slice-start.1 = ((s8[4718592]{0:T(1024)(128)(4,1)}), s8[524288]{0:T(1024)(128)(4,1)S(1)}, s32[]{:S(2)}) async-start(s8[4718592]{0:T(1024)(128)(4,1)} %bitcast.24), calls=%async_computation.1 | async-start | bytes 1048576
  182.1 114.9 %collective-permute-start.5 = (bf16[768,768]{1,0:T(8,128)(2,1)}, bf16[768,768]{1,0:T(8,128)(2,1)}, u32[]{:S(2)}, u32[]{:S(2)}) collective-permute-start(bf16[768,768]{1,0:T(8,128)(2,1)} %constant_dynamic-slice_fusion.13), channel_id=1, source_target_pairs={{0,2},{1,3},{2,0},{3,1},{4,6},{5,7},{6,4},{7,5},{8,10},{9,11},{10,... | collective-permute-start | bytes 3538952 | tf_op jit(solution)/shard_map/ppermute | solution.py:451
  187.1 4.8 copy-start.1
  188.3 113.1 %collective-permute-start.25 = (bf16[768,768]{1,0:T(8,128)(2,1)}, bf16[768,768]{1,0:T(8,128)(2,1)}, u32[]{:S(2)}, u32[]{:S(2)}) collective-permute-start(bf16[768,768]{1,0:T(8,128)(2,1)} %constant_dynamic-slice_fusion.3), channel_id=1, source_target_pairs={{0,2},{1,3},{2,0},{3,1},{4,6},{5,7},{6,4},{7,5},{8,10},{9,11},{10,... | collective-permute-start | bytes 3538952 | tf_op jit(solution)/shard_map/ppermute | solution.py:451
  191.9 1.9 copy-start.7
  191.9 4.5 copy-start.12
  191.9 4.5 copy-start.11
  192.0 4.5 copy-start.9
  192.0 4.6 copy-start.10
  193.1 110.3 %collective-permute-start.15 = (bf16[768,768]{1,0:T(8,128)(2,1)}, bf16[768,768]{1,0:T(8,128)(2,1)}, u32[]{:S(2)}, u32[]{:S(2)}) collective-permute-start(bf16[768,768]{1,0:T(8,128)(2,1)} %constant_dynamic-slice_fusion.8), channel_id=1, source_target_pairs={{0,2},{1,3},{2,0},{3,1},{4,6},{5,7},{6,4},{7,5},{8,10},{9,11},{10,... | collective-permute-start | bytes 3538952 | tf_op jit(solution)/shard_map/ppermute | solution.py:451
  194.8 252.1 %collective-permute-start.3 = (bf16[2,256,768]{2,1,0:T(8,128)(2,1)}, bf16[2,256,768]{2,1,0:T(8,128)(2,1)}, u32[]{:S(2)}, u32[]{:S(2)}) collective-permute-start(bf16[2,256,768]{2,1,0:T(8,128)(2,1)} %bitcast.14), channel_id=1, source_target_pairs={{0,16},{16,0},{1,17},{17,1},{2,18},{18,2},{3,19},{19,3},{4,20},{20... | collective-permute-start | bytes 2359304 | tf_op jit(solution)/shard_map/ppermute | solution.py:451
  297.0 4.5 copy-start.2
  299.1 16.6 %collective-permute-start.6 = (bf16[384,768]{1,0:T(8,128)(2,1)S(1)}, bf16[384,768]{1,0:T(8,128)(2,1)S(1)}, u32[]{:S(2)}, u32[]{:S(2)}) collective-permute-start(bf16[384,768]{1,0:T(8,128)(2,1)S(1)} %constant_dynamic-slice_fusion.12), channel_id=1, source_target_pairs={{0,16},{16,0},{1,17},{17,1},{2,18},{18,2},{3,19},{19,3},{4,20},{20... | collective-permute-start | bytes 1769480 | tf_op jit(solution)/shard_map/ppermute | solution.py:451
  303.1 25.2 %collective-permute-start.26 = (bf16[384,768]{1,0:T(8,128)(2,1)S(1)}, bf16[384,768]{1,0:T(8,128)(2,1)S(1)}, u32[]{:S(2)}, u32[]{:S(2)}) collective-permute-start(bf16[384,768]{1,0:T(8,128)(2,1)S(1)} %constant_dynamic-slice_fusion.2), channel_id=1, source_target_pairs={{0,16},{16,0},{1,17},{17,1},{2,18},{18,2},{3,19},{19,3},{4,20},{20... | collective-permute-start | bytes 1769480 | tf_op jit(solution)/shard_map/ppermute | solution.py:451
  305.0 33.8 %collective-permute-start.16 = (bf16[384,768]{1,0:T(8,128)(2,1)S(1)}, bf16[384,768]{1,0:T(8,128)(2,1)S(1)}, u32[]{:S(2)}, u32[]{:S(2)}) collective-permute-start(bf16[384,768]{1,0:T(8,128)(2,1)S(1)} %constant_dynamic-slice_fusion.7), channel_id=1, source_target_pairs={{0,16},{16,0},{1,17},{17,1},{2,18},{18,2},{3,19},{19,3},{4,20},{20... | collective-permute-start | bytes 1769480 | tf_op jit(solution)/shard_map/ppermute | solution.py:451
  315.9 25.4 %collective-permute-start.7 = (bf16[192,768]{1,0:T(8,128)(2,1)S(1)}, bf16[192,768]{1,0:T(8,128)(2,1)S(1)}, u32[]{:S(2)}, u32[]{:S(2)}) collective-permute-start(bf16[192,768]{1,0:T(8,128)(2,1)S(1)} %constant_dynamic-slice_fusion.11), channel_id=1, source_target_pairs={{0,4},{1,5},{2,6},{3,7},{4,0},{5,1},{6,2},{7,3},{8,12},{9,13},{10,... | collective-permute-start | bytes 884744 | tf_op jit(solution)/shard_map/ppermute | solution.py:451
  328.5 10.9 %collective-permute-start.27 = (bf16[192,768]{1,0:T(8,128)(2,1)S(1)}, bf16[192,768]{1,0:T(8,128)(2,1)S(1)}, u32[]{:S(2)}, u32[]{:S(2)}) collective-permute-start(bf16[192,768]{1,0:T(8,128)(2,1)S(1)} %constant_dynamic-slice_fusion.1), channel_id=1, source_target_pairs={{0,4},{1,5},{2,6},{3,7},{4,0},{5,1},{6,2},{7,3},{8,12},{9,13},{10,... | collective-permute-start | bytes 884744 | tf_op jit(solution)/shard_map/ppermute | solution.py:451
  339.0 14.4 %collective-permute-start.17 = (bf16[192,768]{1,0:T(8,128)(2,1)S(1)}, bf16[192,768]{1,0:T(8,128)(2,1)S(1)}, u32[]{:S(2)}, u32[]{:S(2)}) collective-permute-start(bf16[192,768]{1,0:T(8,128)(2,1)S(1)} %constant_dynamic-slice_fusion.6), channel_id=1, source_target_pairs={{0,4},{1,5},{2,6},{3,7},{4,0},{5,1},{6,2},{7,3},{8,12},{9,13},{10,... | collective-permute-start | bytes 884744 | tf_op jit(solution)/shard_map/ppermute | solution.py:451
  339.6 10.2 %collective-permute-start.28 = (bf16[96,768]{1,0:T(8,128)(2,1)S(1)}, bf16[96,768]{1,0:T(8,128)(2,1)S(1)}, u32[]{:S(2)}, u32[]{:S(2)}) collective-permute-start(bf16[96,768]{1,0:T(8,128)(2,1)S(1)} %constant_dynamic-slice_fusion), channel_id=1, source_target_pairs={{0,8},{1,9},{2,10},{3,11},{4,12},{5,13},{6,14},{7,15},{8,0},{9,1},... | collective-permute-start | bytes 442376 | tf_op jit(solution)/shard_map/ppermute | solution.py:451
  341.4 23.3 %collective-permute-start.8 = (bf16[96,768]{1,0:T(8,128)(2,1)S(1)}, bf16[96,768]{1,0:T(8,128)(2,1)S(1)}, u32[]{:S(2)}, u32[]{:S(2)}) collective-permute-start(bf16[96,768]{1,0:T(8,128)(2,1)S(1)} %constant_dynamic-slice_fusion.10), channel_id=1, source_target_pairs={{0,8},{1,9},{2,10},{3,11},{4,12},{5,13},{6,14},{7,15},{8,0},{9,1},... | collective-permute-start | bytes 442376 | tf_op jit(solution)/shard_map/ppermute | solution.py:451
  349.8 14.7 %collective-permute-start.29 = (bf16[96,768]{1,0:T(8,128)(2,1)S(1)}, bf16[96,768]{1,0:T(8,128)(2,1)S(1)}, u32[]{:S(2)}, u32[]{:S(2)}) collective-permute-start(bf16[96,768]{1,0:T(8,128)(2,1)S(1)} %add_convert_fusion.12), channel_id=1, source_target_pairs={{0,8},{1,9},{2,10},{3,11},{4,12},{5,13},{6,14},{7,15},{8,0},{9,1},... | collective-permute-start | bytes 442376 | tf_op jit(solution)/shard_map/ppermute | solution.py:451
  353.5 15.5 %collective-permute-start.18 = (bf16[96,768]{1,0:T(8,128)(2,1)S(1)}, bf16[96,768]{1,0:T(8,128)(2,1)S(1)}, u32[]{:S(2)}, u32[]{:S(2)}) collective-permute-start(bf16[96,768]{1,0:T(8,128)(2,1)S(1)} %constant_dynamic-slice_fusion.5), channel_id=1, source_target_pairs={{0,8},{1,9},{2,10},{3,11},{4,12},{5,13},{6,14},{7,15},{8,0},{9,1},... | collective-permute-start | bytes 442376 | tf_op jit(solution)/shard_map/ppermute | solution.py:451
  364.6 10.6 %collective-permute-start.30 = (bf16[192,768]{1,0:T(8,128)(2,1)S(1)}, bf16[192,768]{1,0:T(8,128)(2,1)S(1)}, u32[]{:S(2)}, u32[]{:S(2)}) collective-permute-start(bf16[192,768]{1,0:T(8,128)(2,1)S(1)} %pad_maximum_fusion.15), channel_id=1, source_target_pairs={{0,4},{1,5},{2,6},{3,7},{4,0},{5,1},{6,2},{7,3},{8,12},{9,13},{10,... | collective-permute-start | bytes 884744 | tf_op jit(solution)/shard_map/ppermute | solution.py:451
  364.8 12.5 %collective-permute-start.9 = (bf16[96,768]{1,0:T(8,128)(2,1)S(1)}, bf16[96,768]{1,0:T(8,128)(2,1)S(1)}, u32[]{:S(2)}, u32[]{:S(2)}) collective-permute-start(bf16[96,768]{1,0:T(8,128)(2,1)S(1)} %add_convert_fusion.14), channel_id=1, source_target_pairs={{0,8},{1,9},{2,10},{3,11},{4,12},{5,13},{6,14},{7,15},{8,0},{9,1},... | collective-permute-start | bytes 442376 | tf_op jit(solution)/shard_map/ppermute | solution.py:451
  369.0 9.9 %collective-permute-start.19 = (bf16[96,768]{1,0:T(8,128)(2,1)S(1)}, bf16[96,768]{1,0:T(8,128)(2,1)S(1)}, u32[]{:S(2)}, u32[]{:S(2)}) collective-permute-start(bf16[96,768]{1,0:T(8,128)(2,1)S(1)} %add_convert_fusion.13), channel_id=1, source_target_pairs={{0,8},{1,9},{2,10},{3,11},{4,12},{5,13},{6,14},{7,15},{8,0},{9,1},... | collective-permute-start | bytes 442376 | tf_op jit(solution)/shard_map/ppermute | solution.py:451
  375.4 12.0 %collective-permute-start.31 = (bf16[384,768]{1,0:T(8,128)(2,1)S(1)}, bf16[384,768]{1,0:T(8,128)(2,1)S(1)}, u32[]{:S(2)}, u32[]{:S(2)}) collective-permute-start(bf16[384,768]{1,0:T(8,128)(2,1)S(1)} %pad_maximum_fusion.12), channel_id=1, source_target_pairs={{0,16},{16,0},{1,17},{17,1},{2,18},{18,2},{3,19},{19,3},{4,20},{20... | collective-permute-start | bytes 1769480 | tf_op jit(solution)/shard_map/ppermute | solution.py:451
  377.3 18.2 %collective-permute-start.10 = (bf16[192,768]{1,0:T(8,128)(2,1)S(1)}, bf16[192,768]{1,0:T(8,128)(2,1)S(1)}, u32[]{:S(2)}, u32[]{:S(2)}) collective-permute-start(bf16[192,768]{1,0:T(8,128)(2,1)S(1)} %pad_maximum_fusion.13), channel_id=1, source_target_pairs={{0,4},{1,5},{2,6},{3,7},{4,0},{5,1},{6,2},{7,3},{8,12},{9,13},{10,... | collective-permute-start | bytes 884744 | tf_op jit(solution)/shard_map/ppermute | solution.py:451
  378.9 17.4 %collective-permute-start.20 = (bf16[192,768]{1,0:T(8,128)(2,1)S(1)}, bf16[192,768]{1,0:T(8,128)(2,1)S(1)}, u32[]{:S(2)}, u32[]{:S(2)}) collective-permute-start(bf16[192,768]{1,0:T(8,128)(2,1)S(1)} %pad_maximum_fusion.14), channel_id=1, source_target_pairs={{0,4},{1,5},{2,6},{3,7},{4,0},{5,1},{6,2},{7,3},{8,12},{9,13},{10,... | collective-permute-start | bytes 884744 | tf_op jit(solution)/shard_map/ppermute | solution.py:451
  387.7 34.7 %collective-permute-start.32 = (bf16[768,768]{1,0:T(8,128)(2,1)S(1)}, bf16[768,768]{1,0:T(8,128)(2,1)S(1)}, u32[]{:S(2)}, u32[]{:S(2)}) collective-permute-start(bf16[768,768]{1,0:T(8,128)(2,1)S(1)} %pad_maximum_fusion.9), channel_id=1, source_target_pairs={{0,2},{1,3},{2,0},{3,1},{4,6},{5,7},{6,4},{7,5},{8,10},{9,11},{10,... | collective-permute-start | bytes 3538952 | tf_op jit(solution)/shard_map/ppermute | solution.py:451
  395.7 10.5 %collective-permute-start.11 = (bf16[384,768]{1,0:T(8,128)(2,1)S(1)}, bf16[384,768]{1,0:T(8,128)(2,1)S(1)}, u32[]{:S(2)}, u32[]{:S(2)}) collective-permute-start(bf16[384,768]{1,0:T(8,128)(2,1)S(1)} %pad_maximum_fusion.10), channel_id=1, source_target_pairs={{0,16},{16,0},{1,17},{17,1},{2,18},{18,2},{3,19},{19,3},{4,20},{20... | collective-permute-start | bytes 1769480 | tf_op jit(solution)/shard_map/ppermute | solution.py:451
  396.5 27.9 %collective-permute-start.21 = (bf16[384,768]{1,0:T(8,128)(2,1)S(1)}, bf16[384,768]{1,0:T(8,128)(2,1)S(1)}, u32[]{:S(2)}, u32[]{:S(2)}) collective-permute-start(bf16[384,768]{1,0:T(8,128)(2,1)S(1)} %pad_maximum_fusion.11), channel_id=1, source_target_pairs={{0,16},{16,0},{1,17},{17,1},{2,18},{18,2},{3,19},{19,3},{4,20},{20... | collective-permute-start | bytes 1769480 | tf_op jit(solution)/shard_map/ppermute | solution.py:451
  406.5 39.8 %collective-permute-start.12 = (bf16[768,768]{1,0:T(8,128)(2,1)S(1)}, bf16[768,768]{1,0:T(8,128)(2,1)S(1)}, u32[]{:S(2)}, u32[]{:S(2)}) collective-permute-start(bf16[768,768]{1,0:T(8,128)(2,1)S(1)} %pad_maximum_fusion.7), channel_id=1, source_target_pairs={{0,2},{1,3},{2,0},{3,1},{4,6},{5,7},{6,4},{7,5},{8,10},{9,11},{10,... | collective-permute-start | bytes 3538952 | tf_op jit(solution)/shard_map/ppermute | solution.py:451
  422.9 1.4 copy-start.6
  423.0 39.5 %collective-permute-start.33 = (bf16[1536,768]{1,0:T(8,128)(2,1)S(1)}, bf16[1536,768]{1,0:T(8,128)(2,1)S(1)}, u32[]{:S(2)}, u32[]{:S(2)}) collective-permute-start(bf16[1536,768]{1,0:T(8,128)(2,1)S(1)} %pad_maximum_fusion.2), channel_id=1, source_target_pairs={{0,1},{1,0},{2,3},{3,2},{4,5},{5,4},{6,7},{7,6},{8,9},{9,8},{10,11... | collective-permute-start | bytes 7077896 | tf_op jit(solution)/shard_map/ppermute | solution.py:451
  424.4 22.5 %collective-permute-start.2 = (bf16[2,256,768]{2,1,0:T(8,128)(2,1)S(1)}, bf16[2,256,768]{2,1,0:T(8,128)(2,1)S(1)}, u32[]{:S(2)}, u32[]{:S(2)}) collective-permute-start(bf16[2,256,768]{2,1,0:T(8,128)(2,1)S(1)} %bitcast.38), channel_id=1, source_target_pairs={{0,16},{16,0},{1,17},{17,1},{2,18},{18,2},{3,19},{19,3},{4,20},{20... | collective-permute-start | bytes 2359304 | tf_op jit(solution)/shard_map/ppermute | solution.py:451
  424.8 37.0 %collective-permute-start.22 = (bf16[768,768]{1,0:T(8,128)(2,1)S(1)}, bf16[768,768]{1,0:T(8,128)(2,1)S(1)}, u32[]{:S(2)}, u32[]{:S(2)}) collective-permute-start(bf16[768,768]{1,0:T(8,128)(2,1)S(1)} %pad_maximum_fusion.8), channel_id=1, source_target_pairs={{0,2},{1,3},{2,0},{3,1},{4,6},{5,7},{6,4},{7,5},{8,10},{9,11},{10,... | collective-permute-start | bytes 3538952 | tf_op jit(solution)/shard_map/ppermute | solution.py:451
  446.8 17.0 %collective-permute-start.13 = (bf16[1536,768]{1,0:T(8,128)(2,1)S(1)}, bf16[1536,768]{1,0:T(8,128)(2,1)S(1)}, u32[]{:S(2)}, u32[]{:S(2)}) collective-permute-start(bf16[1536,768]{1,0:T(8,128)(2,1)S(1)} %pad_maximum_fusion), channel_id=1, source_target_pairs={{0,1},{1,0},{2,3},{3,2},{4,5},{5,4},{6,7},{7,6},{8,9},{9,8},{10,11... | collective-permute-start | bytes 7077896 | tf_op jit(solution)/shard_map/ppermute | solution.py:451
  462.4 7.1 %collective-permute-start.23 = (bf16[1536,768]{1,0:T(8,128)(2,1)S(1)}, bf16[1536,768]{1,0:T(8,128)(2,1)}, u32[]{:S(2)}, u32[]{:S(2)}) collective-permute-start(bf16[1536,768]{1,0:T(8,128)(2,1)S(1)} %pad_maximum_fusion.1), channel_id=1, source_target_pairs={{0,1},{1,0},{2,3},{3,2},{4,5},{5,4},{6,7},{7,6},{8,9},{9,8},{10,11... | collective-permute-start | bytes 7077896 | tf_op jit(solution)/shard_map/ppermute | solution.py:451
